TPU v7x, 256 devices: a whole 4x4x8 slice. The times are simulated.
256 devices in a mesh: uly: 16 (over z_lo, y), blk: 16 (over z_hi, x, core).
Axes of the slice: x: 4, y: 4, z: 8 (z_hi: 2, z_lo: 4; z = z_hi * 4 + z_lo), core: 2. Of those that a mesh axis runs over, the one named last changes fastest.
Arguments:
- queries: bfloat16 [8192, 5120], P(('blk', 'uly')), may hold values from -60 to 60
- keys: bfloat16 [8192, 5120], P(('blk', 'uly')), may hold values from -9 to 9
- values: bfloat16 [8192, 5120], P(('blk', 'uly')), may hold values from -6 to 6
- row_counts: int32 [16], replicated, may hold values from 64 to 448, as said below
Outputs:
- attended: bfloat16 [8192, 4096], P(('blk', 'uly'))
- leftover_rows: bfloat16 [114688, 128], P(('blk', 'uly'))
Inputs may be any that keep to these rules, and one draw needn't show every extreme that they name: `row_counts`: entry u counts the query rows of leftover head 32 + u // 2 that device u of each uly group serves; the 2 consecutive entries of one head sum to 512; some entry equals 448.
All inputs are finite; a program needn't handle non-finite values.
Results may differ from a plain program's by a relative error of at most 0.0095.
Values may be sent and summed in bfloat16 or wider, within the bound.
A program may use at most 64 MiB of HBM per device.

v0:
```python
import jax
import jax.numpy as jnp
from jax import lax
from jax.sharding import PartitionSpec as P

HEAD_DIM = 128
MAIN = 32
LEFT = 8


def online_update(state, query_rows, key_block, value_block):
    best, totals, weighted = state
    scores = jnp.einsum(
        "qhd,khd->qhk", query_rows, key_block, preferred_element_type=jnp.float32
    ) * HEAD_DIM ** (-0.5)
    new_best = jnp.maximum(best, jnp.max(scores, axis=2))
    factor = jnp.exp(best - new_best)
    expon = jnp.exp(scores - new_best[:, :, None])
    totals = totals * factor + jnp.sum(expon, axis=2)
    update = jnp.einsum(
        "qhk,khd->qhd", expon.astype(jnp.bfloat16), value_block, preferred_element_type=jnp.float32
    )
    weighted = weighted * factor[:, :, None] + update
    return (new_best, totals, weighted)


def fold_blocks(state, query_rows, key_piece, value_piece, block_rows):
    count_blocks = key_piece.shape[0] // block_rows
    width_heads = key_piece.shape[1]
    keys_split = key_piece.reshape(count_blocks, block_rows, width_heads, HEAD_DIM)
    values_split = value_piece.reshape(count_blocks, block_rows, width_heads, HEAD_DIM)

    def step_fn(carry, pair):
        return (online_update(carry, query_rows, pair[0], pair[1]), None)

    state, unused = lax.scan(step_fn, state, (keys_split, values_split))
    return state


def empty_state(query_count, width_heads):
    best = jnp.full((query_count, width_heads), -1e30, jnp.float32)
    totals = jnp.zeros((query_count, width_heads), jnp.float32)
    weighted = jnp.zeros((query_count, width_heads, HEAD_DIM), jnp.float32)
    return (best, totals, weighted)


def per_device(queries, keys, values, row_counts):
    uly_size = lax.axis_size("uly")
    tok_rows = queries.shape[0]
    group_rows = tok_rows * uly_size
    per_head = uly_size // LEFT
    main_per = MAIN // uly_size
    most_rows = group_rows - (per_head - 1) * (group_rows // 8)
    main_cols = MAIN * HEAD_DIM

    def split_heads(field):
        main_part = field[:, :main_cols].reshape(tok_rows, uly_size, main_per * HEAD_DIM)
        rest_part = field[:, main_cols:].reshape(tok_rows, LEFT, HEAD_DIM)
        rest_part = jnp.repeat(rest_part, per_head, axis=1)
        return (main_part, rest_part)

    main_q, rest_q = split_heads(queries)
    main_k, rest_k = split_heads(keys)
    main_v, rest_v = split_heads(values)
    moved_main = (
        lax.all_to_all(main_q, "uly", split_axis=1, concat_axis=0, tiled=True),
        lax.all_to_all(main_k, "uly", split_axis=1, concat_axis=0, tiled=True),
        lax.all_to_all(main_v, "uly", split_axis=1, concat_axis=0, tiled=True),
    )
    moved_rest = (
        lax.all_to_all(rest_q, "uly", split_axis=1, concat_axis=0, tiled=True),
        lax.all_to_all(rest_k, "uly", split_axis=1, concat_axis=0, tiled=True),
        lax.all_to_all(rest_v, "uly", split_axis=1, concat_axis=0, tiled=True),
    )
    head_q = moved_main[0].reshape(group_rows, main_per, HEAD_DIM)
    head_k = moved_main[1].reshape(group_rows, main_per, HEAD_DIM)
    head_v = moved_main[2].reshape(group_rows, main_per, HEAD_DIM)
    left_q = moved_rest[0]
    left_k = moved_rest[1]
    left_v = moved_rest[2]
    device_pos = lax.axis_index("uly")
    within_pair = device_pos % per_head
    exclusive = jnp.cumsum(row_counts) - row_counts
    positions = jnp.arange(uly_size, dtype=jnp.int32)
    mine_count = jnp.sum(jnp.where(positions == device_pos, row_counts, 0))
    mine_excl = jnp.sum(jnp.where(positions == device_pos, exclusive, 0))
    first_excl = jnp.sum(jnp.where(positions == device_pos - within_pair, exclusive, 0))
    row_start = mine_excl - first_excl
    padded_q = jnp.pad(left_q, ((0, most_rows), (0, 0), (0, 0)))
    chosen_q = lax.dynamic_slice_in_dim(padded_q, row_start, most_rows, 0)
    main_init = empty_state(group_rows, main_per)
    left_init = empty_state(most_rows, 1)
    piece = (
        lax.all_gather(head_k, "blk", axis=0, tiled=True),
        lax.all_gather(head_v, "blk", axis=0, tiled=True),
    )
    main_final = fold_blocks(main_init, head_q, piece[0], piece[1], group_rows)
    piece = (
        lax.all_gather(left_k, "blk", axis=0, tiled=True),
        lax.all_gather(left_v, "blk", axis=0, tiled=True),
    )
    left_final = fold_blocks(left_init, chosen_q, piece[0], piece[1], group_rows)
    main_out = (main_final[2] / main_final[1][:, :, None]).astype(jnp.bfloat16)
    attended = lax.all_to_all(
        main_out.reshape(group_rows, main_per * HEAD_DIM),
        "uly",
        split_axis=0,
        concat_axis=1,
        tiled=True,
    )
    left_out = (left_final[2][:, 0, :] / left_final[1]).astype(jnp.bfloat16)
    offsets = jnp.arange(most_rows, dtype=jnp.int32)
    leftover_rows = jnp.where(offsets[:, None] < mine_count, left_out, jnp.zeros_like(left_out))
    return (attended, leftover_rows)


def solution(mesh):
    placed = (P(("blk", "uly"), None), P(("blk", "uly"), None), P(("blk", "uly"), None), P())
    return jax.shard_map(
        per_device,
        mesh=mesh,
        in_specs=placed,
        out_specs=(P(("blk", "uly"), None), P(("blk", "uly"), None)),
        check_vma=False,
    )
```

profile of v0, /device:TPU:1, one launch (start us, length us, event | category | flops | bytes accessed | tf_op | source)
XLA Modules:
  0.0 360.4 jit_solution(5390685024415189760)
XLA Ops:
  8.3 18.6 %all_to_all.118 = bf16[32,16,256]{2,0,1:T(8,128)(2,1)S(1)} all-to-all(bf16[32,16,256]{2,0,1:T(8,128)(2,1)S(1)} %bitcast.187), channel_id=1, replica_groups=mesh['uly'=16,'blk'=16] {'uly'}, dimensions={1} | all-to-all | bytes 524288 | tf_op jit(solution)/shard_map/all_to_all | solution.py:67
  27.8 12.9 %all_to_all.119 = bf16[32,16,256]{2,0,1:T(8,128)(2,1)S(1)} all-to-all(bf16[32,16,256]{2,0,1:T(8,128)(2,1)S(1)} %bitcast.189), channel_id=1, replica_groups=mesh['uly'=16,'blk'=16] {'uly'}, dimensions={1} | all-to-all | bytes 524288 | tf_op jit(solution)/shard_map/all_to_all | solution.py:68
  42.4 12.4 %all_to_all.120 = bf16[32,16,128]{2,0,1:T(8,128)(2,1)} all-to-all(bf16[32,16,128]{2,0,1:T(8,128)(2,1)S(1)} %bitcast.197), channel_id=1, replica_groups=mesh['uly'=16,'blk'=16] {'uly'}, dimensions={1} | all-to-all | bytes 262144 | tf_op jit(solution)/shard_map/all_to_all | solution.py:72
  55.6 3.5 all-to-all-start.5
  59.2 7.7 %all-to-all-done.5 = bf16[32,16,128]{2,0,1:T(8,128)(2,1)S(1)} async-done(((bf16[32,16,128]{2,0,1:T(8,128)(2,1)}), bf16[32,16,128]{2,0,1:T(8,128)(2,1)S(1)}, u32[]{:S(2)}, u32[]{:S(2)}) %all-to-all-start.5) | async-done | bytes 131104 | tf_op jit(solution)/shard_map/all_to_all | solution.py:71
  67.6 3.5 all-to-all-start.6
  71.8 14.7 %all-to-all-done.6 = bf16[32,16,128]{2,0,1:T(8,128)(2,1)S(1)} async-done(((bf16[32,16,128]{2,0,1:T(8,128)(2,1)}), bf16[32,16,128]{2,0,1:T(8,128)(2,1)S(1)}, u32[]{:S(2)}, u32[]{:S(2)}) %all-to-all-start.6) | async-done | bytes 131104 | tf_op jit(solution)/shard_map/all_to_all | solution.py:73
  86.5 13.7 %all-to-all-start.1 = ((bf16[32,16,256]{2,0,1:T(8,128)(2,1)}), bf16[32,16,256]{2,0,1:T(8,128)(2,1)S(1)}, u32[]{:S(2)}, u32[]{:S(2)}) async-start(bf16[32,16,256]{2,0,1:T(8,128)(2,1)} %bitcast.145), calls=%async_computation.1 | async-start | bytes 524288 | tf_op jit(solution)/shard_map/all_to_all | solution.py:66
  103.4 5.7 %all-to-all-done.1 = bf16[32,16,256]{2,0,1:T(8,128)(2,1)S(1)} async-done(((bf16[32,16,256]{2,0,1:T(8,128)(2,1)}), bf16[32,16,256]{2,0,1:T(8,128)(2,1)S(1)}, u32[]{:S(2)}, u32[]{:S(2)}) %all-to-all-start.1) | async-done | bytes 262176 | tf_op jit(solution)/shard_map/all_to_all | solution.py:66
  109.2 74.1 %all-gather.7.cloned.1.call-done = bf16[8192,2,128]{2,1,0:T(2,128)(2,1)} async-done(((bf16[512,2,128]{2,1,0:T(2,128)(2,1)}), bf16[8192,2,128]{2,1,0:T(2,128)(2,1)}) %all-gather.7.cloned.1.call-update) | async-done | bytes 4194320 | tf_op jit(solution)/shard_map/all_gather | solution.py:95
  183.3 49.2 %while.30 = (s32[]{:T(128)}, f32[512,2]{0,1:T(2,128)S(1)}, f32[512,2]{0,1:T(2,128)S(1)}, f32[512,2,128]{0,2,1:T(8,128)S(1)}, bf16[16,512,2,128]{3,2,1,0:T(2,128)...) while((s32[]{:T(128)}, f32[512,2]{0,1:T(2,128)S(1)}, ...), condition=%wide.region_3.4_spmd.clone, body=%wide.region_0.0_spmd.clone.sunk | while | flops 273028096 | bytes 9764981 | solution.py:36
  183.3 1.4 constant_dynamic-slice_fusion.3
  186.4 1.4 constant_dynamic-slice_fusion.3
  189.5 1.4 constant_dynamic-slice_fusion.3
  192.5 1.4 constant_dynamic-slice_fusion.3
  195.6 1.4 constant_dynamic-slice_fusion.3
  198.7 1.4 constant_dynamic-slice_fusion.3
  201.7 1.4 constant_dynamic-slice_fusion.3
  204.8 1.4 constant_dynamic-slice_fusion.3
  207.9 1.4 constant_dynamic-slice_fusion.3
  210.9 1.4 constant_dynamic-slice_fusion.3
  214.0 1.4 constant_dynamic-slice_fusion.3
  217.0 1.5 constant_dynamic-slice_fusion.3
  220.2 1.4 constant_dynamic-slice_fusion.3
  223.3 1.4 constant_dynamic-slice_fusion.3
  226.4 1.4 constant_dynamic-slice_fusion.3
  229.4 1.4 constant_dynamic-slice_fusion.3
  233.6 4.0 %all-to-all-start.3 = ((bf16[16,32,256]{2,1,0:T(8,128)(2,1)}), bf16[16,32,256]{2,1,0:T(8,128)(2,1)S(1)}, u32[]{:S(2)}, u32[]{:S(2)}) async-start(bf16[16,32,256]{2,1,0:T(8,128)(2,1)} %all_to_all.95), calls=%async_computation.3 | async-start | bytes 524288 | tf_op jit(solution)/shard_map/all_to_all | solution.py:104
  237.6 7.0 %all-gather.9.cloned.1.call-done = bf16[8192,1,128]{2,0,1:T(8,128)(2,1)} async-done(((bf16[512,1,128]{2,0,1:T(8,128)(2,1)}), bf16[8192,1,128]{2,0,1:T(8,128)(2,1)}) %all-gather.9.cloned.1.call-update) | async-done | bytes 2097168 | tf_op jit(solution)/shard_map/all_gather | solution.py:99
  244.6 61.2 %all-gather.11.cloned.1.call-done = bf16[8192,1,128]{2,0,1:T(8,128)(2,1)} async-done(((bf16[512,1,128]{2,0,1:T(8,128)(2,1)}), bf16[8192,1,128]{2,0,1:T(8,128)(2,1)}) %all-gather.11.cloned.1.call-update) | async-done | bytes 2097168 | tf_op jit(solution)/shard_map/all_gather | solution.py:100
  305.7 46.6 %while.31 = (s32[]{:T(128)}, f32[448,1]{0,1:T(1,128)S(1)}, f32[448,1]{0,1:T(1,128)S(1)}, f32[448,1,128]{2,0,1:T(8,128)S(1)}, bf16[16,512,1,128]{3,1,2,0:T(8,128)...) while((s32[]{:T(128)}, f32[448,1]{0,1:T(1,128)S(1)}, ...), condition=%wide.region_11.12_spmd.clone, body=%wide.region_8.11_spmd.clone.sunk | while | flops 118991040 | bytes 3616889 | solution.py:36
  308.6 1.3 fusion.59
  (262 shorter events, 80.8 us)
Async XLA Ops:
  7.2 20.6 %slice-start = ((bf16[32,5120]{1,0:T(8,128)(2,1)}), bf16[32,4096]{1,0:T(8,128)(2,1)S(1)}, s32[]{:S(2)}) async-start(bf16[32,5120]{1,0:T(8,128)(2,1)} %param.10), calls=%async_computation.11 | async-start | bytes 524288 | tf_op jit(solution)/shard_map/slice | solution.py:57
  7.2 102.0 %all-gather.5.cloned.1.call-start = ((), (), s32[]{:S(2)}) async-start(), calls=%async_computation.7 | async-start | bytes 4456448 | tf_op jit(solution)/shard_map/all_gather | solution.py:94
  8.3 46.7 %copy-start.2 = (bf16[32,5120]{1,0:T(8,128)(2,1)S(1)}, bf16[32,5120]{1,0:T(8,128)(2,1)}, u32[]{:S(2)}) copy-start(bf16[32,5120]{1,0:T(8,128)(2,1)} %param.8) | copy-start | bytes 983044
  27.6 31.5 %copy-start.1 = (bf16[32,5120]{1,0:T(8,128)(2,1)S(1)}, bf16[32,5120]{1,0:T(8,128)(2,1)}, u32[]{:S(2)}) copy-start(bf16[32,5120]{1,0:T(8,128)(2,1)} %param.10) | copy-start | bytes 983044
  27.7 155.7 %all-gather.7.cloned.1.call-start = ((), (), s32[]{:S(2)}) async-start(), calls=%async_computation.8 | async-start | bytes 4456448 | tf_op jit(solution)/shard_map/all_gather | solution.py:95
  27.7 43.3 %slice-start.1 = ((bf16[32,5120]{1,0:T(8,128)(2,1)}), bf16[32,4096]{1,0:T(8,128)(2,1)S(1)}, s32[]{:S(2)}) async-start(bf16[32,5120]{1,0:T(8,128)(2,1)} %param.8), calls=%async_computation.12 | async-start | bytes 524288 | tf_op jit(solution)/shard_map/slice | solution.py:57
  40.7 59.6 %copy-start.4 = (s32[16]{0:T(128)S(1)}, s32[16]{0:T(128)}, u32[]{:S(2)}) copy-start(s32[16]{0:T(128)} %param.11) | copy-start | bytes 196
  41.5 203.1 %all-gather.9.cloned.1.call-start = ((), (), s32[]{:S(2)}) async-start(), calls=%async_computation.9 | async-start | bytes 2228224 | tf_op jit(solution)/shard_map/all_gather | solution.py:99
  55.6 11.3 %all-to-all-start.5 = ((bf16[32,16,128]{2,0,1:T(8,128)(2,1)}), bf16[32,16,128]{2,0,1:T(8,128)(2,1)S(1)}, u32[]{:S(2)}, u32[]{:S(2)}) async-start(bf16[32,16,128]{2,0,1:T(8,128)(2,1)} %bitcast.15), calls=%async_computation.5 | async-start | bytes 262144 | tf_op jit(solution)/shard_map/all_to_all | solution.py:71
  67.6 19.0 %all-to-all-start.6 = ((bf16[32,16,128]{2,0,1:T(8,128)(2,1)}), bf16[32,16,128]{2,0,1:T(8,128)(2,1)S(1)}, u32[]{:S(2)}, u32[]{:S(2)}) async-start(bf16[32,16,128]{2,0,1:T(8,128)(2,1)} %bitcast.20), calls=%async_computation.6 | async-start | bytes 262144 | tf_op jit(solution)/shard_map/all_to_all | solution.py:73
  86.5 16.6 %copy-start.3 = (bf16[32,16,128]{2,0,1:T(8,128)(2,1)}, bf16[32,16,128]{2,0,1:T(8,128)(2,1)S(1)}, u32[]{:S(2)}) copy-start(bf16[32,16,128]{2,0,1:T(8,128)(2,1)S(1)} %all-to-all-done.6) | copy-start | bytes 393220
  86.5 22.5 %all-to-all-start.1 = ((bf16[32,16,256]{2,0,1:T(8,128)(2,1)}), bf16[32,16,256]{2,0,1:T(8,128)(2,1)S(1)}, u32[]{:S(2)}, u32[]{:S(2)}) async-start(bf16[32,16,256]{2,0,1:T(8,128)(2,1)} %bitcast.145), calls=%async_computation.1 | async-start | bytes 524288 | tf_op jit(solution)/shard_map/all_to_all | solution.py:66
  100.2 205.5 %all-gather.11.cloned.1.call-start = ((), (), s32[]{:S(2)}) async-start(), calls=%async_computation.10 | async-start | bytes 2228224 | tf_op jit(solution)/shard_map/all_gather | solution.py:100
  232.5 73.2 %copy-start = (f32[448,1,128]{2,0,1:T(8,128)S(1)}, f32[448,1,128]{2,0,1:T(8,128)}, u32[]{:S(2)}) copy-start(f32[448,1,128]{2,0,1:T(8,128)} %custom-call.5) | copy-start | bytes 688132
  233.6 119.6 %all-to-all-start.3 = ((bf16[16,32,256]{2,1,0:T(8,128)(2,1)}), bf16[16,32,256]{2,1,0:T(8,128)(2,1)S(1)}, u32[]{:S(2)}, u32[]{:S(2)}) async-start(bf16[16,32,256]{2,1,0:T(8,128)(2,1)} %all_to_all.95), calls=%async_computation.3 | async-start | bytes 524288 | tf_op jit(solution)/shard_map/all_to_all | solution.py:104
Sparse Core Ops, SparseCore 0:
  27.8 79.5 all-gather.4
  110.1 73.1 all-gather.6
  186.1 58.4 all-gather.8
  247.2 58.5 all-gather.10
where the time goes:
time: 362 us; the launch traced here: 360 us
  waiting for transfers between devices  170 us (47%)
  matrix products  57.4 us (16%)
  blocking collectives  44 us (12%)
  local copies, waits for them, and re-layouts  32.9 us (9%)
  starting transfers between devices  24.8 us (7%)
  between operations  15.2 us (4%)
  other arithmetic  14 us (4%)
    all_gather x1, waiting for transfers between devices, per_device(): lax.all_gather(head_v, 'blk', axis=0, tiled=True)  74.1 us
    all_gather x1, waiting for transfers between devices, per_device(): lax.all_gather(left_v, 'blk', axis=0, tiled=True)  61.2 us
    dot_general x32, matrix products, online_update(): jnp.einsum('qhk,khd->qhd', expon.astype(jnp.bfloat16), value_block, prefe...  29.7 us
    dot_general x32, matrix products, online_update(): jnp.einsum('qhd,khd->qhk', query_rows, key_block, preferred_element_type=...  27.8 us
    dynamic_slice x32, local copies, waits for them, and re-layouts, fold_blocks(): state, unused = lax.scan(step_fn, state, (keys_split, values_split))  25.1 us
    all_to_all x1, blocking collectives, per_device(): lax.all_to_all(main_k, 'uly', split_axis=1, concat_axis=0, tiled=True)  18.6 us
    all_to_all x1, waiting for transfers between devices, per_device(): lax.all_to_all(rest_v, 'uly', split_axis=1, concat_axis=0, tiled=True)  14.7 us
    all_to_all x1, starting transfers between devices, per_device(): lax.all_to_all(main_q, 'uly', split_axis=1, concat_axis=0, tiled=True)  13.7 us
  transfers between devices with their start and end apart: 8, of which 6 were waited for; matrix products, arithmetic and copies ran while one was open for 28% of the time, Pallas kernels for 0%

commit v1 on v0

v1 whole, which is shorter than its diff:
```python
import functools

import jax
import jax.numpy as jnp
from jax import lax
from jax.experimental import pallas as pl
from jax.experimental.pallas import tpu as pltpu
from jax.sharding import PartitionSpec as P

ZH, ZL, NY, NX = 2, 4, 4, 4
NZ = ZH * ZL
NP = NZ * NY
TOK = 32
D = 128
ROWS = 3 * TOK
MOST = 448
MAIN = 0
LEFT = 1
QB = 256
EXP2_SCALE = D ** (-0.5) * 1.4426950408889634


def kernel(
    counts_ref, q_ref, k_ref, v_ref, att_ref, left_ref,
    send_main, send_left, kv, acc, top, out_main, out_left, got_main, got_left,
    s1m_send, s1m_recv, s1l_send, s1l_recv, yg_send, yg_recv,
    x_send, x_recv, c_send, c_recv, lo_send, lo_recv, om_send, om_recv,
):
    u = lax.axis_index("uly")
    b = lax.axis_index("blk")
    y = lax.rem(u, NY)
    zl = u // NY
    c = lax.rem(b, 2)
    x = lax.rem(b // 2, NX)
    zh = b // (2 * NX)
    z = zh * ZL + zl
    me = z * NY + y
    right = lax.rem(x + 1, NX)
    left = lax.rem(x + NX - 1, NX)
    far = lax.rem(x + 2, NX)

    def dev(x_, c_, z_, y_):
        return {"uly": lax.rem(z_, ZL) * NY + y_, "blk": ((z_ // ZL) * NX + x_) * 2 + c_}

    def dev_p(p):
        return dev(x, c, p // NY, lax.rem(p, NY))

    def remote(src, dst, ss, rs, to):
        return pltpu.make_async_remote_copy(
            src_ref=src, dst_ref=dst, send_sem=ss, recv_sem=rs,
            device_id=to, device_id_type=pl.DeviceIdType.MESH,
        )

    barrier = pltpu.get_barrier_semaphore()

    def greet(i, _):
        pl.semaphore_signal(barrier, inc=1, device_id=dev_p(lax.rem(me + i, NP)),
                            device_id_type=pl.DeviceIdType.MESH)
        return 0

    lax.fori_loop(1, NP, greet, 0)
    for to in (dev(right, c, z, y), dev(left, c, z, y), dev(x, 1 - c, z, y)):
        pl.semaphore_signal(barrier, inc=1, device_id=to, device_id_type=pl.DeviceIdType.MESH)

    for zz in range(NZ):
        head = NP + (zz % ZL) * (NY // 2) + zz // ZL
        for n, ref in enumerate((q_ref, k_ref, v_ref)):
            send_left[zz, n * TOK:(n + 1) * TOK, :] = ref[:, head * D:(head + 1) * D]
    pl.semaphore_wait(barrier, NP - 1 + 3)

    def send_l(i, _):
        to = lax.rem(z + i, NZ)
        remote(send_left.at[to], kv.at[c, x, LEFT, y * NZ + z], s1l_send.at[to], s1l_recv.at[z],
               dev(x, c, to, y)).start()
        return 0

    lax.fori_loop(1, NZ, send_l, 0)
    for p in range(NP):
        for n, ref in enumerate((q_ref, k_ref, v_ref)):
            send_main[p, n * TOK:(n + 1) * TOK, :] = ref[:, p * D:(p + 1) * D]

    def send_m(i, _):
        to = lax.rem(me + i, NP)
        remote(send_main.at[to], kv.at[c, x, MAIN, me], s1m_send.at[to], s1m_recv.at[me],
               dev_p(to)).start()
        return 0

    lax.fori_loop(1, NP, send_m, 0)
    kv[c, x, LEFT, y * NZ + z] = send_left[z]
    kv[c, x, MAIN, me] = send_main[me]
    acc[...] = jnp.zeros_like(acc)
    top[...] = jnp.full_like(top, -1e30)

    def wait_l(i, _):
        frm = lax.rem(z + i, NZ)
        remote(send_left.at[frm], kv.at[c, x, LEFT, y * NZ + frm], s1l_send.at[frm],
               s1l_recv.at[frm], dev(x, c, frm, y)).wait_recv()
        return 0

    lax.fori_loop(1, NZ, wait_l, 0)

    def yg(src_y, to_y, sem_s):
        part = kv.at[c, x, LEFT, pl.ds(src_y * NZ, NZ), pl.ds(TOK, 2 * TOK)]
        return remote(part, part, yg_send.at[sem_s], yg_recv.at[src_y], dev(x, c, z, to_y))

    for i in range(1, NY):
        to = lax.rem(y + i, NY)
        yg(y, to, to).start()
    for i in range(1, NY):
        frm = lax.rem(y + i, NY)
        yg(frm, frm, frm).wait_recv()

    def part_of(cc, xx, h, lo, n):
        return kv.at[cc, xx, h, pl.ds(lo, n), pl.ds(TOK, 2 * TOK)]

    half = NP // 2

    def x_copy(h, kind, xx, to):
        lo, n = ((0, NP), (0, NP), (0, half), (half, half))[kind]
        part = part_of(c, xx, h, lo, n)
        return remote(part, part, x_send.at[h, kind], x_recv.at[h, kind], dev(to, c, z, y))

    def c_copy(h, k, cc, xx):
        part = part_of(cc, xx, h, 0, NP)
        return remote(part, part, c_send.at[h, k], c_recv.at[h, k], dev(x, 1 - c, z, y))

    def start_own(h):
        x_copy(h, 0, x, right).start()
        x_copy(h, 1, x, left).start()
        c_copy(h, 0, c, x).start()

    def attend(h, cc, xx, row, count):
        def block(i, _):
            at = pl.multiple_of(i * QB, QB)
            src = i * (QB // TOK)
            if h == LEFT:
                src = src + y * NZ
            qq = kv[c, x, h, pl.ds(src, QB // TOK), 0:TOK, :].reshape(QB, D)
            kk = kv[cc, xx, h, :, TOK:2 * TOK, :].reshape(NP * TOK, D)
            vv = kv[cc, xx, h, :, 2 * TOK:3 * TOK, :].reshape(NP * TOK, D)
            at = at + row
            s = lax.dot_general(qq, kk, (((1,), (1,)), ((), ())), preferred_element_type=jnp.float32)
            before = top[pl.ds(at, QB), :]
            now = jnp.maximum(before, jnp.max(s, axis=1, keepdims=True))
            factor = jnp.exp2((before - now) * EXP2_SCALE)
            w = jnp.exp2((s - now[:, :1]) * EXP2_SCALE)
            top[pl.ds(at, QB), :] = now
            ones = jnp.concatenate([vv, jnp.ones_like(vv)], axis=1)
            o = jnp.dot(w.astype(jnp.bfloat16), ones, preferred_element_type=jnp.float32)
            acc[pl.ds(at, QB), :D] = acc[pl.ds(at, QB), :D] * factor + o[:, :D]
            acc[pl.ds(at, QB), D:] = acc[pl.ds(at, QB), D:] * factor + o[:, D:]
            return 0

        lax.fori_loop(0, count, block, 0, unroll=min(count, 4))

    def one_head(h, row, count, middle):
        def step(t, _):
            @pl.when(t == 1)
            def _():
                c_copy(h, 0, 1 - c, x).wait_recv()

            @pl.when(t == 2)
            def _():
                x_copy(h, 0, left, right).wait_recv()
                x_copy(h, 2, left, right).start()
                c_copy(h, 1, c, left).start()
                x_copy(h, 1, right, left).wait_recv()
                x_copy(h, 3, right, left).start()
                c_copy(h, 2, c, right).start()
                middle()

            @pl.when(t == 4)
            def _():
                c_copy(h, 1, 1 - c, left).wait_recv()
                c_copy(h, 2, 1 - c, right).wait_recv()

            @pl.when(t == 6)
            def _():
                x_copy(h, 2, far, right).wait_recv()
                x_copy(h, 3, far, left).wait_recv()
                c_copy(h, 3, c, far).start()

            @pl.when(t == 7)
            def _():
                c_copy(h, 3, 1 - c, far).wait_recv()

            flip = jnp.where((t == 1) | (t == 4) | (t == 5) | (t == 7), 1, 0)
            xx = jnp.where(t < 2, x, jnp.where(t > 5, far, jnp.where(lax.rem(t, 2) == 0, left, right)))
            attend(h, jnp.where(flip == 1, 1 - c, c), xx, row, count)
            return 0

        lax.fori_loop(0, 8, step, 0)

    def wait_m(i, _):
        frm = lax.rem(me + i, NP)
        remote(send_main.at[frm], kv.at[c, x, MAIN, frm], s1m_send.at[frm], s1m_recv.at[frm],
               dev_p(frm)).wait_recv()
        return 0

    def main_ready():
        lax.fori_loop(1, NP, wait_m, 0)
        start_own(MAIN)

    n_main = NP * TOK
    n_left = NZ * TOK
    start_own(LEFT)
    one_head(LEFT, n_main, n_left // QB, main_ready)

    res = acc[n_main:, :D] / acc[n_main:, D:]
    out_left[...] = res.astype(jnp.bfloat16).reshape(NZ, TOK, D)

    def lo_copy(zz, k):
        return remote(out_left.at[pl.ds(zz * ZL, ZL)], got_left.at[y], lo_send.at[2 * zz + k],
                      lo_recv.at[y], dev(x, c, zz * ZL + zl, 2 * zh + k))

    for zz in range(ZH):
        for k in range(2):
            own = (zz == zh) & (2 * zh + k == y)

            @pl.when(own)
            def _():
                got_left[y] = out_left[zz * ZL:(zz + 1) * ZL]

            @pl.when(jnp.logical_not(own))
            def _():
                lo_copy(zz, k).start()

    one_head(MAIN, 0, n_main // QB, lambda: None)
    res = acc[:n_main, :D] / acc[:n_main, D:]
    out_main[...] = res.astype(jnp.bfloat16).reshape(NP, TOK, D)

    def send_o(i, _):
        to = lax.rem(me + i, NP)
        remote(out_main.at[to], got_main.at[me], om_send.at[to], om_recv.at[me], dev_p(to)).start()
        return 0

    lax.fori_loop(1, NP, send_o, 0)
    got_main[me] = out_main[me]

    pair = y // 2
    for yy in range(NY):
        @pl.when(jnp.logical_not((pair == zh) & (yy == y)))
        def _():
            remote(out_left.at[pl.ds(0, ZL)], got_left.at[yy], lo_send.at[0], lo_recv.at[yy],
                   dev(x, c, pair * ZL + zl, yy)).wait_recv()
    group = ZL * NY * TOK
    mine = counts_ref[u]
    first = jnp.where(lax.rem(u, 2) == 1, counts_ref[u - lax.rem(u, 2)], 0)
    col = lax.broadcasted_iota(jnp.int32, (MOST, group), 1)
    row = lax.broadcasted_iota(jnp.int32, (MOST, group), 0)
    piece = col // TOK
    place = (lax.rem(piece, ZL) * NY + piece // ZL) * TOK + lax.rem(col, TOK)
    pick = (place == row + first) & (row < mine)
    pick = jnp.where(pick, 1.0, 0.0).astype(jnp.bfloat16)
    left_ref[...] = jnp.dot(pick, got_left[...].reshape(group, D),
                            preferred_element_type=jnp.float32).astype(jnp.bfloat16)

    def wait_o(i, _):
        frm = lax.rem(me + i, NP)
        remote(out_main.at[frm], got_main.at[frm], om_send.at[frm], om_recv.at[frm],
               dev_p(frm)).wait_recv()
        return 0

    lax.fori_loop(1, NP, wait_o, 0)
    for p in range(NP):
        att_ref[:, p * D:(p + 1) * D] = got_main[p]

    def sent_l(i, _):
        to = lax.rem(z + i, NZ)
        remote(send_left.at[to], kv.at[c, x, LEFT, y * NZ + z], s1l_send.at[to], s1l_recv.at[z],
               dev(x, c, to, y)).wait_send()
        return 0

    lax.fori_loop(1, NZ, sent_l, 0)

    def sent_m(i, _):
        to = lax.rem(me + i, NP)
        remote(send_main.at[to], kv.at[c, x, MAIN, me], s1m_send.at[to], s1m_recv.at[me],
               dev_p(to)).wait_send()
        remote(out_main.at[to], got_main.at[me], om_send.at[to], om_recv.at[me],
               dev_p(to)).wait_send()
        return 0

    lax.fori_loop(1, NP, sent_m, 0)
    for i in range(1, NY):
        to = lax.rem(y + i, NY)
        yg(y, to, to).wait_send()
    for h in (MAIN, LEFT):
        x_copy(h, 0, x, right).wait_send()
        x_copy(h, 1, x, left).wait_send()
        x_copy(h, 2, left, right).wait_send()
        x_copy(h, 3, right, left).wait_send()
        for k, xx in enumerate((x, left, right, far)):
            c_copy(h, k, c, xx).wait_send()
    for zz in range(ZH):
        for k in range(2):
            @pl.when(jnp.logical_not((zz == zh) & (2 * zh + k == y)))
            def _():
                lo_copy(zz, k).wait_send()


def per_device(queries, keys, values, row_counts):
    group = ZL * NY * TOK
    vmem = pl.BlockSpec(memory_space=pltpu.VMEM)
    rows = NP * TOK + NZ * TOK
    dma = pltpu.SemaphoreType.DMA
    bf, f32 = jnp.bfloat16, jnp.float32
    flops = 4 * rows * NX * 2 * NP * TOK * D
    return pl.pallas_call(
        kernel,
        out_shape=(
            jax.ShapeDtypeStruct((TOK, NP * D), bf),
            jax.ShapeDtypeStruct((MOST, D), bf),
        ),
        in_specs=[pl.BlockSpec(memory_space=pltpu.SMEM), vmem, vmem, vmem],
        out_specs=(vmem, vmem),
        scratch_shapes=[
            pltpu.VMEM((NP, ROWS, D), bf),
            pltpu.VMEM((NZ, ROWS, D), bf),
            pltpu.VMEM((2, NX, 2, NP, ROWS, D), bf),
            pltpu.VMEM((rows, 2 * D), f32),
            pltpu.VMEM((rows, D), f32),
            pltpu.VMEM((NP, TOK, D), bf),
            pltpu.VMEM((NZ, TOK, D), bf),
            pltpu.VMEM((NP, TOK, D), bf),
            pltpu.VMEM((NY, ZL, TOK, D), bf),
            dma((NP,)), dma((NP,)), dma((NZ,)), dma((NZ,)), dma((NY,)), dma((NY,)),
            dma((2, 4)), dma((2, 4)), dma((2, 4)), dma((2, 4)),
            dma((2 * ZH,)), dma((NY,)), dma((NP,)), dma((NP,)),
        ],
        compiler_params=pltpu.CompilerParams(
            collective_id=0, has_side_effects=True, vmem_limit_bytes=48 * 2 ** 20
        ),
        cost_estimate=pl.CostEstimate(flops=flops, bytes_accessed=2 ** 22, transcendentals=flops // 512),
    )(row_counts, queries, keys, values)


def solution(mesh):
    placed = (P(("blk", "uly"), None), P(("blk", "uly"), None), P(("blk", "uly"), None), P())
    return jax.shard_map(
        per_device,
        mesh=mesh,
        in_specs=placed,
        out_specs=(P(("blk", "uly"), None), P(("blk", "uly"), None)),
        check_vma=False,
    )
```

time: 362 us -> 90.9 us (0.25)
  waiting for transfers between devices: 170 us -> 0 us
  Pallas kernels: 0 us -> 85.2 us
  matrix products: 57.4 us -> 0 us
  blocking collectives: 44 us -> 0 us
  local copies, waits for them, and re-layouts: 32.9 us -> 4.92 us
  starting transfers between devices: 24.8 us -> 0 us
  between operations: 15.2 us -> 0.65 us
  other arithmetic: 14 us -> 0 us
    all_gather x4 -> x0, waiting for transfers between devices: 142 us -> none  [the longest x1 74.1 us: per_device(): lax.all_gather(head_v, 'blk', axis=0, tiled=True)]
    pallas_call x0 -> x1, Pallas kernels: none -> 85.2 us  [per_device(): pl.pallas_call(kernel, out_shape=(jax.ShapeDtypeStruct((TOK, NP * D), bf)...]
    dot_general x64 -> x0, matrix products: 57.4 us -> none  [the longest x32 29.7 us: online_update(): jnp.einsum('qhk,khd->qhd', expon.astype(jnp.bfloat16), value_block, prefe...]
    all_to_all x3 -> x0, blocking collectives: 44 us -> none  [the longest x1 18.6 us: per_device(): lax.all_to_all(main_k, 'uly', split_axis=1, concat_axis=0, tiled=True)]
    all_to_all x4 -> x0, waiting for transfers between devices: 28.1 us -> none  [the longest x1 14.7 us: per_device(): lax.all_to_all(rest_v, 'uly', split_axis=1, concat_axis=0, tiled=True)]
    dynamic_slice x33 -> x0, local copies, waits for them, and re-layouts: 25.3 us -> none  [the longest x32 25.1 us: fold_blocks(): state, unused = lax.scan(step_fn, state, (keys_split, values_split))]
    all_to_all x4 -> x0, starting transfers between devices: 24.7 us -> none  [the longest x1 13.7 us: per_device(): lax.all_to_all(main_q, 'uly', split_axis=1, concat_axis=0, tiled=True)]
    reduce_sum x33 -> x0, other arithmetic: 11.4 us -> none  [the longest x32 10.7 us: online_update(): totals = totals * factor + jnp.sum(expon, axis=2)]
  transfers between devices with their start and end apart: 8 -> 0, of which waited for: 6 -> 0; matrix products, arithmetic and copies ran while one was open for 28% -> 0% of each run, Pallas kernels for 0% -> 0%
where the time goes in v1:
time: 90.9 us; the launch traced here: 90.7 us
  Pallas kernels  85.2 us (94%)
  local copies, waits for them, and re-layouts  4.92 us (5%)
    pallas_call x1, Pallas kernels, per_device(): pl.pallas_call(kernel, out_shape=(jax.ShapeDtypeStruct((TOK, NP * D), bf)...  85.2 us
    unnamed x10, local copies, waits for them, and re-layouts  4.92 us

profile of v1, /device:TPU:1, one launch (start us, length us, event | category | flops | bytes accessed | tf_op | source)
XLA Modules:
  0.0 90.7 jit_solution(1222606898537383959)
XLA Ops:
  0.6 0.0 copy-start
  0.6 1.0 %copy-done = bf16[32,5120]{1,0:T(8,128)(2,1)S(1)} copy-done((bf16[32,5120]{1,0:T(8,128)(2,1)S(1)}, bf16[32,5120]{1,0:T(8,128)(2,1)}, u32[]{:S(2)}) %copy-start) | copy-done | bytes 327704
  1.6 0.0 copy-start.1
  1.6 1.0 %copy-done.1 = bf16[32,5120]{1,0:T(8,128)(2,1)S(1)} copy-done((bf16[32,5120]{1,0:T(8,128)(2,1)S(1)}, bf16[32,5120]{1,0:T(8,128)(2,1)}, u32[]{:S(2)}) %copy-start.1) | copy-done | bytes 327704
  2.6 0.0 copy-start.2
  2.6 1.0 %copy-done.2 = bf16[32,5120]{1,0:T(8,128)(2,1)S(1)} copy-done((bf16[32,5120]{1,0:T(8,128)(2,1)S(1)}, bf16[32,5120]{1,0:T(8,128)(2,1)}, u32[]{:S(2)}) %copy-start.2) | copy-done | bytes 327704
  3.6 0.0 copy-start.3
  3.6 0.7 copy-done.3
  4.2 85.2 %shard_map.59 = (bf16[32,4096]{1,0:T(8,128)(2,1)S(1)}, bf16[448,128]{1,0:T(8,128)(2,1)S(1)}) custom-call(s32[16]{0:T(128)S(1)} %copy-done.3, bf16[32,5120]{1,0:T(8,128)(2,1)S(1)} %copy-done, bf16[32,5120]{1,0:T(8,128)(2,1)S(1)} %copy-done.1, bf16[32,5120]{1,0:T(8,128)(2,1)S(1)} %copy-done.2), custom_call_target="tpu_custom_call" | custom-call | flops 5368709120 | bytes 4194304 | tf_op jit(solution)/shard_map/pallas_call | solution.py:309
  89.4 0.7 copy.8
  90.1 0.6 copy.9
Async XLA Ops:
  0.6 1.0 %copy-start = (bf16[32,5120]{1,0:T(8,128)(2,1)S(1)}, bf16[32,5120]{1,0:T(8,128)(2,1)}, u32[]{:S(2)}) copy-start(bf16[32,5120]{1,0:T(8,128)(2,1)} %q_ref.1) | copy-start | bytes 983044
  1.6 1.0 %copy-start.1 = (bf16[32,5120]{1,0:T(8,128)(2,1)S(1)}, bf16[32,5120]{1,0:T(8,128)(2,1)}, u32[]{:S(2)}) copy-start(bf16[32,5120]{1,0:T(8,128)(2,1)} %k_ref.1) | copy-start | bytes 983044
  2.6 1.0 %copy-start.2 = (bf16[32,5120]{1,0:T(8,128)(2,1)S(1)}, bf16[32,5120]{1,0:T(8,128)(2,1)}, u32[]{:S(2)}) copy-start(bf16[32,5120]{1,0:T(8,128)(2,1)} %v_ref.1) | copy-start | bytes 983044
  3.6 0.7 copy-start.3

commit v2 on v1

v2 whole, which is shorter than its diff:
```python
import jax
import jax.numpy as jnp
from jax import lax
from jax.experimental import pallas as pl
from jax.experimental.pallas import tpu as pltpu
from jax.sharding import PartitionSpec as P

ZH, ZL, NY, NX = 2, 4, 4, 4
NZ = ZH * ZL
NP = NZ * NY
TOK = 32
D = 128
MOST = 448
QB = 256
LB = 64
EXP2_SCALE = D ** (-0.5) * 1.4426950408889634
MESH = pl.DeviceIdType.MESH


def kernel(
    counts_ref, q_ref, k_ref, v_ref, att_ref, left_ref,
    kvm, kvl, qm, ql, acc, top, out_main, out_left, got_left,
    s1_send, s1_recv, m_send, m_recv, mc_send, mc_recv,
    lx_send, lx_recv, ly_send, ly_recv, lc_send, lc_recv,
    lo_send, lo_recv, om_send, om_recv,
):
    u = lax.axis_index("uly")
    b = lax.axis_index("blk")
    y = lax.rem(u, NY)
    zl = u // NY
    c = lax.rem(b, 2)
    x = lax.rem(b // 2, NX)
    zh = b // (2 * NX)
    z = zh * ZL + zl
    me = z * NY + y
    half = NP // 2
    n_main = NP * TOK

    def dev(x_, c_, z_, y_):
        return {"uly": lax.rem(z_, ZL) * NY + y_, "blk": ((z_ // ZL) * NX + x_) * 2 + c_}

    def dev_p(p):
        return dev(x, c, p // NY, lax.rem(p, NY))

    def remote(src, dst, ss, rs, to):
        return pltpu.make_async_remote_copy(
            src_ref=src, dst_ref=dst, send_sem=ss, recv_sem=rs,
            device_id=to, device_id_type=MESH,
        )

    def ring(at, size):
        return lax.rem(at + 1, size), lax.rem(at + size - 1, size), lax.rem(at + 2, size)

    xr, xl, xf = ring(x, NX)
    yr, yl, yf = ring(y, NY)

    barrier = pltpu.get_barrier_semaphore()

    def greet(i, _):
        pl.semaphore_signal(barrier, inc=1, device_id=dev_p(lax.rem(me + i, NP)), device_id_type=MESH)
        return 0

    lax.fori_loop(1, NP, greet, 0)
    for to in (dev(xr, c, z, y), dev(xl, c, z, y), dev(x, 1 - c, z, y)):
        pl.semaphore_signal(barrier, inc=1, device_id=to, device_id_type=MESH)

    def columns(ref, head):
        return ref.at[:, pl.ds(pl.multiple_of(head * D, D), D)]

    def left_head(zz):
        return NP + lax.rem(zz, ZL) * (NY // 2) + zz // ZL

    own_a = 1 // (NZ // 2)
    own_at = NY % half
    own = [
        pltpu.make_async_copy(columns(k_ref, left_head(z)), kvl.at[y, c, x, z, pl.ds(0, TOK)], s1_recv.at[2]),
        pltpu.make_async_copy(columns(v_ref, left_head(z)), kvl.at[y, c, x, z, pl.ds(TOK, TOK)], s1_recv.at[2]),
        pltpu.make_async_copy(columns(k_ref, me), kvm.at[x, own_a, c, own_at + y, pl.ds(0, TOK)], s1_recv.at[own_a]),
        pltpu.make_async_copy(columns(v_ref, me), kvm.at[x, own_a, c, own_at + y, pl.ds(TOK, TOK)], s1_recv.at[own_a]),
        pltpu.make_async_copy(columns(q_ref, me), qm.at[me], s1_recv.at[3]),
        pltpu.make_async_copy(columns(q_ref, left_head(z)), ql.at[z], s1_recv.at[4]),
    ]
    for copy in own:
        copy.start()
    acc[...] = jnp.zeros_like(acc)
    top[...] = jnp.full_like(top, -1e30)
    pl.semaphore_wait(barrier, NP - 1 + 3)

    def send_lkv(i, _):
        to = lax.rem(z + i, NZ)
        for n, ref in enumerate((k_ref, v_ref)):
            remote(columns(ref, left_head(to)), kvl.at[y, c, x, z, pl.ds(n * TOK, TOK)],
                   s1_send.at[0], s1_recv.at[2], dev(x, c, to, y)).start()
        return 0

    def send_lq(i, _):
        to = lax.rem(z + i, NZ)
        remote(columns(q_ref, left_head(to)), ql.at[z], s1_send.at[1], s1_recv.at[4],
               dev(x, c, to, y)).start()
        return 0

    def send_mkv(chunk):
        def send(i, _):
            rel = i // NY
            to_z = lax.rem(z - rel + 1 + NZ, NZ)
            to_y = lax.rem(y + lax.rem(i, NY), NY)
            slot = lax.rem(rel, NZ // 2) * NY + y
            for n, ref in enumerate((k_ref, v_ref)):
                remote(columns(ref, to_z * NY + to_y), kvm.at[x, chunk, c, slot, pl.ds(n * TOK, TOK)],
                       s1_send.at[2 + n], s1_recv.at[chunk], dev(x, c, to_z, to_y)).start()
            return 0

        lo, hi = chunk * half, (chunk + 1) * half
        if lo <= NY < hi:
            lax.fori_loop(lo, NY, send, 0)
            lax.fori_loop(NY + 1, hi, send, 0)
        else:
            lax.fori_loop(lo, hi, send, 0)

    def send_mq(i, _):
        to = lax.rem(me + i, NP)
        remote(columns(q_ref, to), qm.at[me], s1_send.at[4], s1_recv.at[3], dev_p(to)).start()
        return 0

    lax.fori_loop(1, NZ, send_lkv, 0)
    send_mkv(0)
    lax.fori_loop(1, NZ, send_lq, 0)
    lax.fori_loop(1, NP, send_mq, 0)
    send_mkv(1)

    def landed(ref, sem):
        pltpu.make_async_copy(ref, ref, sem).wait()

    def m_copy(a, kind, xx, to):
        lo, n = ((0, half), (0, half), (0, half // 2), (half // 2, half // 2))[kind]
        part = kvm.at[xx, a, c, pl.ds(lo, n)]
        return remote(part, part, m_send.at[a, kind], m_recv.at[a, kind], dev(to, c, z, y))

    def mc_copy(a, k, cc, xx):
        part = kvm.at[xx, a, cc]
        return remote(part, part, mc_send.at[a, k], mc_recv.at[a, k], dev(x, 1 - c, z, y))

    def lx_copy(kind, xx, to):
        lo, n = ((0, NZ), (0, NZ), (0, NZ // 2), (NZ // 2, NZ // 2))[kind]
        part = kvl.at[y, c, xx, pl.ds(lo, n)]
        return remote(part, part, lx_send.at[kind], lx_recv.at[kind], dev(to, c, z, y))

    def ly_copy(kind, yy, to):
        lo, n = ((0, NX), (0, NX), (0, NX // 2), (NX // 2, NX // 2))[kind]
        part = kvl.at[yy, c, pl.ds(lo, n)]
        return remote(part, part, ly_send.at[kind], ly_recv.at[kind], dev(x, c, z, to))

    def lc_copy(k, cc, yy):
        part = kvl.at[yy, cc]
        return remote(part, part, lc_send.at[k], lc_recv.at[k], dev(x, 1 - c, z, y))

    def main_own(a):
        landed(kvm.at[x, a, c], s1_recv.at[a])
        m_copy(a, 0, x, xr).start()
        m_copy(a, 1, x, xl).start()
        mc_copy(a, 0, c, x).start()

    def main_pass(a):
        m_copy(a, 0, xl, xr).wait_recv()
        m_copy(a, 2, xl, xr).start()
        mc_copy(a, 1, c, xl).start()
        m_copy(a, 1, xr, xl).wait_recv()
        m_copy(a, 3, xr, xl).start()
        mc_copy(a, 2, c, xr).start()

    def main_far(a):
        m_copy(a, 2, xf, xr).wait_recv()
        m_copy(a, 3, xf, xl).wait_recv()
        mc_copy(a, 3, c, xf).start()

    def update(qq, kk, vv, at, n):
        s = lax.dot_general(qq, kk, (((1,), (1,)), ((), ())), preferred_element_type=jnp.float32)
        before = top[pl.ds(at, n), :]
        now = jnp.maximum(before, jnp.max(s, axis=1, keepdims=True))
        factor = jnp.exp2((before - now) * EXP2_SCALE)
        w = jnp.exp2((s - now[:, :1]) * EXP2_SCALE)
        top[pl.ds(at, n), :] = now
        ones = jnp.concatenate([vv, jnp.ones_like(vv)], axis=1)
        o = jnp.dot(w.astype(jnp.bfloat16), ones, preferred_element_type=jnp.float32)
        acc[pl.ds(at, n), :D] = acc[pl.ds(at, n), :D] * factor + o[:, :D]
        acc[pl.ds(at, n), D:] = acc[pl.ds(at, n), D:] * factor + o[:, D:]

    def attend_main(xx, a):
        def block(i, _):
            at = pl.multiple_of(i * QB, QB)
            qq = qm[pl.ds(i * (QB // TOK), QB // TOK)].reshape(QB, D)
            kk = kvm[xx, a, :, :, 0:TOK, :].reshape(NP * TOK, D)
            vv = kvm[xx, a, :, :, TOK:2 * TOK, :].reshape(NP * TOK, D)
            update(qq, kk, vv, at, QB)
            return 0

        lax.fori_loop(0, n_main // QB, block, 0, unroll=min(n_main // QB, 4))

    def attend_left(yy):
        def block(i, _):
            at = pl.multiple_of(n_main + i * LB, LB)
            qq = ql[pl.ds(i * (LB // TOK), LB // TOK)].reshape(LB, D)
            kk = kvl[yy, :, :, :, 0:TOK, :].reshape(2 * NX * NZ * TOK, D)
            vv = kvl[yy, :, :, :, TOK:2 * TOK, :].reshape(2 * NX * NZ * TOK, D)
            update(qq, kk, vv, at, LB)
            return 0

        count = NZ * TOK // LB
        lax.fori_loop(0, count, block, 0, unroll=min(count, 4))

    landed(kvl.at[y, c, x], s1_recv.at[2])
    lx_copy(0, x, xr).start()
    lx_copy(1, x, xl).start()
    main_own(0)
    lx_copy(0, xl, xr).wait_recv()
    lx_copy(2, xl, xr).start()
    lx_copy(1, xr, xl).wait_recv()
    lx_copy(3, xr, xl).start()
    lx_copy(2, xf, xr).wait_recv()
    lx_copy(3, xf, xl).wait_recv()
    ly_copy(0, y, yr).start()
    if NY > 2:
        ly_copy(1, y, yl).start()
    lc_copy(0, c, y).start()
    main_pass(0)
    landed(qm, s1_recv.at[3])
    landed(ql, s1_recv.at[4])

    def step(t, _):
        @pl.when(t == 0)
        def _():
            mc_copy(0, 0, 1 - c, x).wait_recv()

        @pl.when(t == 1)
        def _():
            ly_copy(0, yl, yr).wait_recv()
            lc_copy(1, c, yl).start()
            if NY > 2:
                ly_copy(2, yl, yr).start()
                ly_copy(1, yr, yl).wait_recv()
                ly_copy(3, yr, yl).start()
                lc_copy(2, c, yr).start()
            main_far(0)
            mc_copy(0, 1, 1 - c, xl).wait_recv()

        @pl.when(t == 2)
        def _():
            main_own(1)
            mc_copy(0, 2, 1 - c, xr).wait_recv()

        @pl.when(t == 3)
        def _():
            mc_copy(0, 3, 1 - c, xf).wait_recv()

        @pl.when(t == 4)
        def _():
            if NY > 2:
                ly_copy(2, yf, yr).wait_recv()
                ly_copy(3, yf, yl).wait_recv()
                lc_copy(3, c, yf).start()
            mc_copy(1, 0, 1 - c, x).wait_recv()

        @pl.when(t == 5)
        def _():
            main_pass(1)
            mc_copy(1, 1, 1 - c, xl).wait_recv()

        @pl.when(t == 6)
        def _():
            main_far(1)
            mc_copy(1, 2, 1 - c, xr).wait_recv()

        @pl.when(t == 7)
        def _():
            mc_copy(1, 3, 1 - c, xf).wait_recv()

        i = lax.rem(t, 4)
        xx = jnp.where(i == 0, x, jnp.where(i == 1, xl, jnp.where(i == 2, xr, xf)))
        attend_main(xx, t // 4)

        def left_step(j, _):
            @pl.when(j == 0)
            def _():
                lc_copy(0, 1 - c, y).wait_recv()

            @pl.when(j == 1)
            def _():
                lc_copy(1, 1 - c, yl).wait_recv()
                if NY > 2:
                    lc_copy(2, 1 - c, yr).wait_recv()

            if NY > 2:
                @pl.when(j == 3)
                def _():
                    lc_copy(3, 1 - c, yf).wait_recv()

            attend_left(jnp.where(j == 0, y, jnp.where(j == 1, yl, jnp.where(j == 2, yr, yf))))
            return 0

        lo = jnp.where(t == 0, 0, jnp.where(t == 2, 1, jnp.where(t == 4, 3, 0)))
        hi = jnp.where(t == 0, 1, jnp.where(t == 2, 3, jnp.where(t == 4, 4, 0)))
        lax.fori_loop(jnp.minimum(lo, NY), jnp.minimum(hi, NY), left_step, 0)

        @pl.when(t == 4)
        def _():
            send_left_out()

        return 0

    def lo_copy(zz, k):
        return remote(out_left.at[pl.ds(zz * ZL, ZL)], got_left.at[y], lo_send.at[2 * zz + k],
                      lo_recv.at[y], dev(x, c, zz * ZL + zl, 2 * zh + k))

    def send_left_out():
        res = acc[n_main:, :D] / acc[n_main:, D:]
        out_left[...] = res.astype(jnp.bfloat16).reshape(NZ, TOK, D)
        for zz in range(ZH):
            for k in range(2):
                own = (zz == zh) & (2 * zh + k == y)

                @pl.when(own)
                def _():
                    got_left[y] = out_left[zz * ZL:(zz + 1) * ZL]

                @pl.when(jnp.logical_not(own))
                def _():
                    lo_copy(zz, k).start()

    lax.fori_loop(0, 8, step, 0)

    res = acc[:n_main, :D] / acc[:n_main, D:]
    out_main[...] = res.astype(jnp.bfloat16).reshape(NP, TOK, D)
    own_out = pltpu.make_async_copy(out_main.at[me], columns(att_ref, me), om_recv)
    own_out.start()

    def send_o(i, _):
        to = lax.rem(me + i, NP)
        remote(out_main.at[to], columns(att_ref, me), om_send, om_recv, dev_p(to)).start()
        return 0

    lax.fori_loop(1, NP, send_o, 0)

    pair = y // 2
    for yy in range(NY):
        @pl.when(jnp.logical_not((pair == zh) & (yy == y)))
        def _():
            remote(out_left.at[pl.ds(0, ZL)], got_left.at[yy], lo_send.at[0], lo_recv.at[yy],
                   dev(x, c, pair * ZL + zl, yy)).wait_recv()
    group = ZL * NY * TOK
    mine = counts_ref[u]
    first = jnp.where(lax.rem(u, 2) == 1, counts_ref[u - lax.rem(u, 2)], 0)
    col = lax.broadcasted_iota(jnp.int32, (MOST, group), 1)
    row = lax.broadcasted_iota(jnp.int32, (MOST, group), 0)
    piece = col // TOK
    place = (lax.rem(piece, ZL) * NY + piece // ZL) * TOK + lax.rem(col, TOK)
    pick = (place == row + first) & (row < mine)
    pick = jnp.where(pick, 1.0, 0.0).astype(jnp.bfloat16)
    left_ref[...] = jnp.dot(pick, got_left[...].reshape(group, D),
                            preferred_element_type=jnp.float32).astype(jnp.bfloat16)

    def sent(ref, sem):
        pltpu.make_async_copy(ref, ref, sem).wait()

    for n in (0, 0, 1):
        sent(qm.at[pl.ds(0, NZ - 1)], s1_send.at[n])
    for n in (2, 3, 4):
        sent(qm.at[pl.ds(0, NP - 1)], s1_send.at[n])
    for a in range(2):
        m_copy(a, 0, x, xr).wait_send()
        m_copy(a, 1, x, xl).wait_send()
        m_copy(a, 2, xl, xr).wait_send()
        m_copy(a, 3, xr, xl).wait_send()
        for k, xx in enumerate((x, xl, xr, xf)):
            mc_copy(a, k, c, xx).wait_send()
    lx_copy(0, x, xr).wait_send()
    lx_copy(1, x, xl).wait_send()
    lx_copy(2, xl, xr).wait_send()
    lx_copy(3, xr, xl).wait_send()
    ly_copy(0, y, yr).wait_send()
    lc_copy(0, c, y).wait_send()
    lc_copy(1, c, yl).wait_send()
    if NY > 2:
        ly_copy(1, y, yl).wait_send()
        ly_copy(2, yl, yr).wait_send()
        ly_copy(3, yr, yl).wait_send()
        lc_copy(2, c, yr).wait_send()
        lc_copy(3, c, yf).wait_send()
    for zz in range(ZH):
        for k in range(2):
            @pl.when(jnp.logical_not((zz == zh) & (2 * zh + k == y)))
            def _():
                lo_copy(zz, k).wait_send()
    landed(qm, om_recv)
    sent(qm.at[pl.ds(0, NP - 1)], om_send)


def per_device(queries, keys, values, row_counts):
    vmem = pl.BlockSpec(memory_space=pltpu.VMEM)
    hbm = pl.BlockSpec(memory_space=pltpu.HBM)
    rows = NP * TOK + NZ * TOK
    dma = pltpu.SemaphoreType.DMA
    bf, f32 = jnp.bfloat16, jnp.float32
    flops = 4 * rows * NX * 2 * NP * TOK * D
    return pl.pallas_call(
        kernel,
        out_shape=(
            jax.ShapeDtypeStruct((TOK, NP * D), bf),
            jax.ShapeDtypeStruct((MOST, D), bf),
        ),
        in_specs=[pl.BlockSpec(memory_space=pltpu.SMEM), hbm, hbm, hbm],
        out_specs=(hbm, vmem),
        scratch_shapes=[
            pltpu.VMEM((NX, 2, 2, NP // 2, 2 * TOK, D), bf),
            pltpu.VMEM((NY, 2, NX, NZ, 2 * TOK, D), bf),
            pltpu.VMEM((NP, TOK, D), bf),
            pltpu.VMEM((NZ, TOK, D), bf),
            pltpu.VMEM((rows, 2 * D), f32),
            pltpu.VMEM((rows, D), f32),
            pltpu.VMEM((NP, TOK, D), bf),
            pltpu.VMEM((NZ, TOK, D), bf),
            pltpu.VMEM((NY, ZL, TOK, D), bf),
            dma((5,)), dma((5,)), dma((2, 4)), dma((2, 4)), dma((2, 4)), dma((2, 4)),
            dma((4,)), dma((4,)), dma((4,)), dma((4,)), dma((4,)), dma((4,)),
            dma((2 * ZH,)), dma((NY,)), dma, dma,
        ],
        compiler_params=pltpu.CompilerParams(
            collective_id=0, has_side_effects=True, vmem_limit_bytes=48 * 2 ** 20
        ),
        cost_estimate=pl.CostEstimate(flops=flops, bytes_accessed=2 ** 22, transcendentals=flops // 512),
    )(row_counts, queries, keys, values)


def solution(mesh):
    placed = (P(("blk", "uly"), None), P(("blk", "uly"), None), P(("blk", "uly"), None), P())
    return jax.shard_map(
        per_device,
        mesh=mesh,
        in_specs=placed,
        out_specs=(P(("blk", "uly"), None), P(("blk", "uly"), None)),
        check_vma=False,
    )
```

time: 90.9 us -> 82.2 us (0.904)
  Pallas kernels: 85.2 us -> 76.4 us
    pallas_call x1, Pallas kernels: 85.2 us -> 76.4 us  [per_device(): pl.pallas_call(kernel, out_shape=(jax.ShapeDtypeStruct((TOK, NP * D), bf)...]
where the time goes in v2:
time: 82.2 us; the launch traced here: 82 us
  Pallas kernels  76.4 us (93%)
  local copies, waits for them, and re-layouts  4.92 us (6%)
    pallas_call x1, Pallas kernels, per_device(): pl.pallas_call(kernel, out_shape=(jax.ShapeDtypeStruct((TOK, NP * D), bf)...  76.4 us
    unnamed x10, local copies, waits for them, and re-layouts  4.92 us

profile of v2, /device:TPU:1, one launch (start us, length us, event | category | flops | bytes accessed | tf_op | source)
XLA Modules:
  0.0 82.0 jit_solution(6253933469612249362)
XLA Ops:
  0.6 0.0 copy-start
  0.6 1.0 %copy-done = bf16[32,5120]{1,0:T(8,128)(2,1)S(1)} copy-done((bf16[32,5120]{1,0:T(8,128)(2,1)S(1)}, bf16[32,5120]{1,0:T(8,128)(2,1)}, u32[]{:S(2)}) %copy-start) | copy-done | bytes 327704
  1.6 0.0 copy-start.1
  1.6 1.0 %copy-done.1 = bf16[32,5120]{1,0:T(8,128)(2,1)S(1)} copy-done((bf16[32,5120]{1,0:T(8,128)(2,1)S(1)}, bf16[32,5120]{1,0:T(8,128)(2,1)}, u32[]{:S(2)}) %copy-start.1) | copy-done | bytes 327704
  2.6 0.0 copy-start.2
  2.6 1.0 %copy-done.2 = bf16[32,5120]{1,0:T(8,128)(2,1)S(1)} copy-done((bf16[32,5120]{1,0:T(8,128)(2,1)S(1)}, bf16[32,5120]{1,0:T(8,128)(2,1)}, u32[]{:S(2)}) %copy-start.2) | copy-done | bytes 327704
  3.6 0.0 copy-start.3
  3.6 0.7 copy-done.3
  4.2 76.4 %shard_map.59 = (bf16[32,4096]{1,0:T(8,128)(2,1)S(1)}, bf16[448,128]{1,0:T(8,128)(2,1)S(1)}) custom-call(s32[16]{0:T(128)S(1)} %copy-done.3, bf16[32,5120]{1,0:T(8,128)(2,1)S(1)} %copy-done, bf16[32,5120]{1,0:T(8,128)(2,1)S(1)} %copy-done.1, bf16[32,5120]{1,0:T(8,128)(2,1)S(1)} %copy-done.2), custom_call_target="tpu_custom_call" | custom-call | flops 5368709120 | bytes 4194304 | tf_op jit(solution)/shard_map/pallas_call | solution.py:404
  80.6 0.7 copy.8
  81.4 0.6 copy.9
Async XLA Ops:
  0.6 1.0 %copy-start = (bf16[32,5120]{1,0:T(8,128)(2,1)S(1)}, bf16[32,5120]{1,0:T(8,128)(2,1)}, u32[]{:S(2)}) copy-start(bf16[32,5120]{1,0:T(8,128)(2,1)} %q_ref.1) | copy-start | bytes 983044
  1.6 1.0 %copy-start.1 = (bf16[32,5120]{1,0:T(8,128)(2,1)S(1)}, bf16[32,5120]{1,0:T(8,128)(2,1)}, u32[]{:S(2)}) copy-start(bf16[32,5120]{1,0:T(8,128)(2,1)} %k_ref.1) | copy-start | bytes 983044
  2.6 1.0 %copy-start.2 = (bf16[32,5120]{1,0:T(8,128)(2,1)S(1)}, bf16[32,5120]{1,0:T(8,128)(2,1)}, u32[]{:S(2)}) copy-start(bf16[32,5120]{1,0:T(8,128)(2,1)} %v_ref.1) | copy-start | bytes 983044
  3.6 0.7 copy-start.3

commit v3 on v0

v3 whole, which is shorter than its diff:
```python
import jax
import jax.numpy as jnp
from jax import lax
from jax.experimental import pallas as pl
from jax.experimental.pallas import tpu as pltpu
from jax.sharding import PartitionSpec as P

ZH, ZL, NY, NX = 2, 4, 4, 4
NZ = ZH * ZL
NP = NZ * NY
TOK = 32
D = 128
MOST = 448
QB = 256
VMEM_LIMIT = 64 * 2 ** 20 - 2 ** 18
EXP2_SCALE = D ** (-0.5) * 1.4426950408889634
MESH = pl.DeviceIdType.MESH


def kernel(
    counts_ref, q_ref, k_ref, v_ref, att_ref, left_ref,
    kv, qs, acc, top, out_main, part_o, part_s, got_o, got_s, out_left, got_left,
    s1_send, s1_recv, m_send, m_recv, mc_send, mc_recv, lx_send, lx_recv, lc_send, lc_recv,
    lq_send, lq_recv, lp_send, lp_recv, lo_send, lo_recv, om_send, om_recv,
):
    u = lax.axis_index("uly")
    b = lax.axis_index("blk")
    y = lax.rem(u, NY)
    zl = u // NY
    c = lax.rem(b, 2)
    x = lax.rem(b // 2, NX)
    zh = b // (2 * NX)
    z = zh * ZL + zl
    me = z * NY + y
    chunks = 4 if NZ == 8 else 2
    order = (0, 1, -1, 2, 3, -2, 4, -3) if NZ == 8 else (0, 1)
    per = NP // chunks
    pairs = chunks // 2
    rows = NP * TOK
    group = NZ * TOK
    left_slot = NX * pairs

    def dev(x_, c_, z_, y_):
        return {"uly": lax.rem(z_, ZL) * NY + y_, "blk": ((z_ // ZL) * NX + x_) * 2 + c_}

    def dev_p(p):
        return dev(x, c, p // NY, lax.rem(p, NY))

    def remote(src, dst, ss, rs, to):
        return pltpu.make_async_remote_copy(
            src_ref=src, dst_ref=dst, send_sem=ss, recv_sem=rs,
            device_id=to, device_id_type=MESH,
        )

    xr, xl, xf = lax.rem(x + 1, NX), lax.rem(x + NX - 1, NX), lax.rem(x + 2, NX)

    barrier = pltpu.get_barrier_semaphore()

    def greet(i, _):
        pl.semaphore_signal(barrier, inc=1, device_id=dev_p(lax.rem(me + i, NP)), device_id_type=MESH)
        return 0

    lax.fori_loop(1, NP, greet, 0)
    for to in (dev(xr, c, z, y), dev(xl, c, z, y), dev(x, 1 - c, z, y)):
        pl.semaphore_signal(barrier, inc=1, device_id=to, device_id_type=MESH)

    def columns(ref, head):
        return ref.at[:, pl.ds(pl.multiple_of(head * D, D), D)]

    def left_head(zz):
        return NP + lax.rem(zz, ZL) * (NY // 2) + zz // ZL

    s_left, s_mq, s_lq = 4, 5, 6

    def main_rows(xx, k, cc, lo, n):
        return kv.at[xx * pairs + k // 2, pl.ds((k % 2) * 2 * per + cc * per + lo, n)]

    def left_rows(cc, xx, lo, n):
        return kv.at[left_slot + cc, pl.ds(xx * NZ + lo, n)]

    def place_main(k, src, n):
        return kv.at[x * pairs + k // 2, (k % 2) * 2 * per + c * per + src, pl.ds(n * TOK, TOK)]

    def place_left(n):
        return kv.at[left_slot + c, x * NZ + z, pl.ds(n * TOK, TOK)]

    own = [
        pltpu.make_async_copy(columns(k_ref, left_head(z)), place_left(0), s1_recv.at[s_left]),
        pltpu.make_async_copy(columns(v_ref, left_head(z)), place_left(1), s1_recv.at[s_left]),
        pltpu.make_async_copy(columns(k_ref, me), place_main(0, y, 0), s1_recv.at[0]),
        pltpu.make_async_copy(columns(v_ref, me), place_main(0, y, 1), s1_recv.at[0]),
        pltpu.make_async_copy(columns(q_ref, me), qs.at[0, me], s1_recv.at[s_mq]),
        pltpu.make_async_copy(columns(q_ref, left_head(z)), qs.at[1, y * NZ + z], s1_recv.at[s_lq]),
    ]
    for copy in own:
        copy.start()
    acc[...] = jnp.zeros_like(acc)
    top[...] = jnp.full_like(top, -1e30)
    pl.semaphore_wait(barrier, NP - 1 + 3)

    def send_lkv(i, _):
        to = lax.rem(z + i, NZ)
        for n, ref in enumerate((k_ref, v_ref)):
            remote(columns(ref, left_head(to)), place_left(n), s1_send.at[0], s1_recv.at[s_left],
                   dev(x, c, to, y)).start()
        return 0

    def send_lq(i, _):
        to = lax.rem(z + i, NZ)
        remote(columns(q_ref, left_head(to)), qs.at[1, y * NZ + z], s1_send.at[1], s1_recv.at[s_lq],
               dev(x, c, to, y)).start()
        return 0

    def send_mkv(k):
        for rel in range(k * per // NY, (k + 1) * per // NY):
            to_z = lax.rem(z - order[rel] + NZ, NZ)
            slot = (rel % (per // NY)) * NY + y

            def send(i, _):
                to_y = lax.rem(y + i, NY)
                for n, ref in enumerate((k_ref, v_ref)):
                    remote(columns(ref, to_z * NY + to_y), place_main(k, slot, n),
                           s1_send.at[2 + n], s1_recv.at[k], dev(x, c, to_z, to_y)).start()
                return 0

            lax.fori_loop(1 if rel == 0 else 0, NY, send, 0)

    def send_mq(i, _):
        to = lax.rem(me + i, NP)
        remote(columns(q_ref, to), qs.at[0, me], s1_send.at[4], s1_recv.at[s_mq], dev_p(to)).start()
        return 0

    lax.fori_loop(1, NZ, send_lkv, 0)
    for k in range(chunks // 2):
        send_mkv(k)
    lax.fori_loop(1, NZ, send_lq, 0)
    lax.fori_loop(1, NP, send_mq, 0)
    for k in range(chunks // 2, chunks):
        send_mkv(k)

    def landed(ref, sem):
        pltpu.make_async_copy(ref, ref, sem).wait()

    def m_copy(k, kind, xx, to):
        lo, n = ((0, per), (0, per), (0, per // 2), (per // 2, per // 2))[kind]
        part = main_rows(xx, k, c, lo, n)
        return remote(part, part, m_send.at[k, kind], m_recv.at[k, kind], dev(to, c, z, y))

    def mc_copy(k, i, cc, xx):
        part = main_rows(xx, k, cc, 0, per)
        return remote(part, part, mc_send.at[k, i], mc_recv.at[k, i], dev(x, 1 - c, z, y))

    def lx_copy(kind, xx, to):
        lo, n = ((0, NZ), (0, NZ), (0, NZ // 2), (NZ // 2, NZ // 2))[kind]
        part = left_rows(c, xx, lo, n)
        return remote(part, part, lx_send.at[kind], lx_recv.at[kind], dev(to, c, z, y))

    def lc_copy(cc):
        part = kv.at[left_slot + cc]
        return remote(part, part, lc_send, lc_recv, dev(x, 1 - c, z, y))

    def lq_copy(src_y, to_y):
        part = qs.at[1, pl.ds(src_y * NZ, NZ)]
        return remote(part, part, lq_send.at[to_y], lq_recv.at[src_y], dev(x, c, z, to_y))

    def lp_copies(src_y, to_y):
        at = pl.ds(pl.multiple_of(to_y * group, group), group)
        return [
            remote(part_o.at[at], got_o.at[src_y], lp_send.at[0, to_y], lp_recv.at[0, src_y], dev(x, c, z, to_y)),
            remote(part_s.at[at], got_s.at[src_y], lp_send.at[1, to_y], lp_recv.at[1, src_y], dev(x, c, z, to_y)),
        ]

    def main_own(k):
        landed(main_rows(x, k, c, 0, per), s1_recv.at[k])
        m_copy(k, 0, x, xr).start()
        m_copy(k, 1, x, xl).start()
        mc_copy(k, 0, c, x).start()

    def main_pass(k):
        m_copy(k, 0, xl, xr).wait_recv()
        m_copy(k, 2, xl, xr).start()
        mc_copy(k, 1, c, xl).start()
        m_copy(k, 1, xr, xl).wait_recv()
        m_copy(k, 3, xr, xl).start()
        mc_copy(k, 2, c, xr).start()

    def main_far(k):
        m_copy(k, 2, xf, xr).wait_recv()
        m_copy(k, 3, xf, xl).wait_recv()
        mc_copy(k, 3, c, xf).start()

    def main_across(pair, i):
        for k in (2 * pair, 2 * pair + 1):
            mc_copy(k, i, 1 - c, (x, xl, xr, xf)[i]).wait_recv()

    def update(head, slot, i):
        at = pl.multiple_of(i * QB, QB)
        if not isinstance(head, int) or head:
            at = pl.multiple_of(head * rows + at, QB)
        n = QB // TOK
        qq = qs[head, pl.ds(i * n, n)].reshape(QB, D)
        kk = kv[slot, :, 0:TOK, :].reshape(4 * per * TOK, D)
        vv = kv[slot, :, TOK:2 * TOK, :].reshape(4 * per * TOK, D)
        s = lax.dot_general(qq, kk, (((1,), (1,)), ((), ())), preferred_element_type=jnp.float32)
        before = top[pl.ds(at, QB), :]
        now = jnp.maximum(before, jnp.max(s, axis=1, keepdims=True))
        factor = jnp.exp2((before - now) * EXP2_SCALE)
        w = jnp.exp2((s - now[:, :1]) * EXP2_SCALE)
        ones = jnp.concatenate([vv, jnp.ones_like(vv)], axis=1)
        o = jnp.dot(w.astype(jnp.bfloat16), ones, preferred_element_type=jnp.float32)
        return at, now, acc[pl.ds(at, QB), :D] * factor + o[:, :D], acc[pl.ds(at, QB), D:] * factor + o[:, D:]

    def attend(head, slot):
        def block(i, _):
            at, now, total, weight = update(head, slot, i)
            top[pl.ds(at, QB), :] = now
            acc[pl.ds(at, QB), :D] = total
            acc[pl.ds(at, QB), D:] = weight
            return 0

        lax.fori_loop(0, rows // QB, block, 0, unroll=True)

    def send_partial():
        at = pl.ds(rows, rows)
        weight = acc[at, D:]
        part_o[...] = (acc[at, :D] / weight).astype(jnp.bfloat16)
        part_s[...] = top[at, :] * EXP2_SCALE + jnp.log2(weight)
        for i in range(1, NY):
            to = lax.rem(y + i, NY)
            for copy in lp_copies(y, to):
                copy.start()
        mine = pl.ds(pl.multiple_of(y * group, group), group)
        got_o[y] = part_o[mine]
        got_s[y] = part_s[mine]

    def lo_copy(zz, k):
        return remote(out_left.at[pl.ds(zz * ZL, ZL)], got_left.at[y], lo_send.at[2 * zz + k],
                      lo_recv.at[y], dev(x, c, zz * ZL + zl, 2 * zh + k))

    def merge_left():
        for i in range(1, NY):
            frm = lax.rem(y + i, NY)
            for copy in lp_copies(frm, frm):
                copy.wait_recv()
        best = got_s[0]
        for yy in range(1, NY):
            best = jnp.maximum(best, got_s[yy])
        total = jnp.zeros((group, D), jnp.float32)
        weight = jnp.zeros((group, D), jnp.float32)
        for yy in range(NY):
            share = jnp.exp2(got_s[yy] - best)
            weight = weight + share
            total = total + share * got_o[yy].astype(jnp.float32)
        out_left[...] = (total / weight).astype(jnp.bfloat16).reshape(NZ, TOK, D)
        for zz in range(ZH):
            for k in range(2):
                here = (zz == zh) & (2 * zh + k == y)

                @pl.when(here)
                def _():
                    got_left[y] = out_left[zz * ZL:(zz + 1) * ZL]

                @pl.when(jnp.logical_not(here))
                def _():
                    lo_copy(zz, k).start()

    landed(left_rows(c, x, 0, NZ), s1_recv.at[s_left])
    lx_copy(0, x, xr).start()
    lx_copy(1, x, xl).start()
    main_own(0)
    lx_copy(0, xl, xr).wait_recv()
    lx_copy(2, xl, xr).start()
    lx_copy(1, xr, xl).wait_recv()
    lx_copy(3, xr, xl).start()
    main_own(1)
    landed(qs.at[1, pl.ds(y * NZ, NZ)], s1_recv.at[s_lq])
    for i in range(1, NY):
        to = lax.rem(y + i, NY)
        lq_copy(y, to).start()
    main_pass(0)
    lx_copy(2, xf, xr).wait_recv()
    lx_copy(3, xf, xl).wait_recv()
    lc_copy(c).start()
    main_pass(1)
    main_far(0)
    landed(qs.at[0], s1_recv.at[s_mq])

    def ready_own(pair):
        main_across(pair, 0)

    def before_left():
        main_far(1)
        for i in range(1, NY):
            frm = lax.rem(y + i, NY)
            lq_copy(frm, frm).wait_recv()

    def before_left_across():
        lc_copy(1 - c).wait_recv()

    xs = (x, xl, xr, xf)
    plan = [
        (0, x * pairs, lambda: main_across(0, 0)),
        (1, left_slot + c, before_left),
        (1, left_slot + 1 - c, before_left_across),
    ]

    def first_neighbour():
        main_across(0, 1)
        send_partial()

    def second_neighbour():
        main_across(0, 2)
        if pairs > 1:
            main_own(2)

    def first_far():
        main_across(0, 3)
        if pairs > 1:
            main_own(3)
            main_pass(2)
        else:
            merge_left()

    plan += [
        (0, xl * pairs, first_neighbour),
        (0, xr * pairs, second_neighbour),
        (0, xf * pairs, first_far),
    ]
    if pairs > 1:
        def second_own():
            merge_left()
            main_far(2)
            main_across(1, 0)

        def second_left():
            main_pass(3)
            main_across(1, 1)

        def second_right():
            main_far(3)
            main_across(1, 2)

        plan += [
            (0, x * pairs + 1, second_own),
            (0, xl * pairs + 1, second_left),
            (0, xr * pairs + 1, second_right),
            (0, xf * pairs + 1, lambda: main_across(1, 3)),
        ]

    def chosen(t, values):
        out = values[0]
        for i in range(1, len(values)):
            out = jnp.where(t == i, values[i], out)
        return out

    def step(t, _):
        for i, (head, slot, first) in enumerate(plan[:-1]):
            pl.when(t == i)(first)
        attend(chosen(t, [p[0] for p in plan[:-1]]), chosen(t, [p[1] for p in plan[:-1]]))
        return 0

    lax.fori_loop(0, len(plan) - 1, step, 0)

    def send_out(p):
        remote(out_main.at[p], columns(att_ref, me), om_send, om_recv, dev_p(p)).start()

    plan[-1][2]()
    parts = 2

    def last(j, _):
        for i in range(rows // QB // parts):
            blk = j * (rows // QB // parts) + i
            at, now, total, weight = update(0, plan[-1][1], blk)
            out_main[pl.ds(blk * (QB // TOK), QB // TOK)] = (
                (total / weight).astype(jnp.bfloat16).reshape(QB // TOK, TOK, D))

        def send(i, _):
            p = j * (NP // parts) + i

            @pl.when(p == me)
            def _():
                pltpu.make_async_copy(out_main.at[me], columns(att_ref, me), om_recv).start()

            @pl.when(p != me)
            def _():
                send_out(p)

            return 0

        lax.fori_loop(0, NP // parts, send, 0)
        return 0

    lax.fori_loop(0, parts, last, 0)

    pair_y = y // 2
    for yy in range(NY):
        @pl.when(jnp.logical_not((pair_y == zh) & (yy == y)))
        def _():
            remote(out_left.at[pl.ds(0, ZL)], got_left.at[yy], lo_send.at[0], lo_recv.at[yy],
                   dev(x, c, pair_y * ZL + zl, yy)).wait_recv()
    block_rows = ZL * NY * TOK
    mine = counts_ref[u]
    first = jnp.where(lax.rem(u, 2) == 1, counts_ref[u - lax.rem(u, 2)], 0)
    col = lax.broadcasted_iota(jnp.int32, (MOST, block_rows), 1)
    row = lax.broadcasted_iota(jnp.int32, (MOST, block_rows), 0)
    piece = col // TOK
    place = (lax.rem(piece, ZL) * NY + piece // ZL) * TOK + lax.rem(col, TOK)
    pick = (place == row + first) & (row < mine)
    pick = jnp.where(pick, 1.0, 0.0).astype(jnp.bfloat16)
    left_ref[...] = jnp.dot(pick, got_left[...].reshape(block_rows, D),
                            preferred_element_type=jnp.float32).astype(jnp.bfloat16)

    for n in (0, 0, 1):
        landed(qs.at[0, pl.ds(0, NZ - 1)], s1_send.at[n])
    for n in (2, 3, 4):
        landed(qs.at[0, pl.ds(0, NP - 1)], s1_send.at[n])
    for k in range(chunks):
        m_copy(k, 0, x, xr).wait_send()
        m_copy(k, 1, x, xl).wait_send()
        m_copy(k, 2, xl, xr).wait_send()
        m_copy(k, 3, xr, xl).wait_send()
        for i in range(4):
            mc_copy(k, i, c, xs[i]).wait_send()
    lx_copy(0, x, xr).wait_send()
    lx_copy(1, x, xl).wait_send()
    lx_copy(2, xl, xr).wait_send()
    lx_copy(3, xr, xl).wait_send()
    lc_copy(c).wait_send()
    for i in range(1, NY):
        to = lax.rem(y + i, NY)
        lq_copy(y, to).wait_send()
        for copy in lp_copies(y, to):
            copy.wait_send()
    for zz in range(ZH):
        for k in range(2):
            @pl.when(jnp.logical_not((zz == zh) & (2 * zh + k == y)))
            def _():
                lo_copy(zz, k).wait_send()
    landed(qs.at[0], om_recv)
    landed(qs.at[0, pl.ds(0, NP - 1)], om_send)


def per_device(queries, keys, values, row_counts):
    vmem = pl.BlockSpec(memory_space=pltpu.VMEM)
    hbm = pl.BlockSpec(memory_space=pltpu.HBM)
    chunks = 4 if NZ == 8 else 2
    rows = NP * TOK
    group = NZ * TOK
    dma = pltpu.SemaphoreType.DMA
    bf, f32 = jnp.bfloat16, jnp.float32
    flops = 4 * rows * (NX * chunks // 2 + 2) * rows * D
    return pl.pallas_call(
        kernel,
        out_shape=(
            jax.ShapeDtypeStruct((TOK, NP * D), bf),
            jax.ShapeDtypeStruct((MOST, D), bf),
        ),
        in_specs=[pl.BlockSpec(memory_space=pltpu.SMEM), hbm, hbm, hbm],
        out_specs=(hbm, vmem),
        scratch_shapes=[
            pltpu.VMEM((NX * chunks // 2 + 2, 4 * NP // chunks, 2 * TOK, D), bf),
            pltpu.VMEM((2, NP, TOK, D), bf),
            pltpu.VMEM((2 * rows, 2 * D), f32),
            pltpu.VMEM((2 * rows, D), f32),
            pltpu.VMEM((NP, TOK, D), bf),
            pltpu.VMEM((rows, D), bf),
            pltpu.VMEM((rows, D), f32),
            pltpu.VMEM((NY, group, D), bf),
            pltpu.VMEM((NY, group, D), f32),
            pltpu.VMEM((NZ, TOK, D), bf),
            pltpu.VMEM((NY, ZL, TOK, D), bf),
            dma((5,)), dma((7,)), dma((4, 4)), dma((4, 4)), dma((4, 4)), dma((4, 4)),
            dma((4,)), dma((4,)), dma, dma,
            dma((NY,)), dma((NY,)), dma((2, NY)), dma((2, NY)), dma((2 * ZH,)), dma((NY,)), dma, dma,
        ],
        compiler_params=pltpu.CompilerParams(
            collective_id=0, has_side_effects=True, vmem_limit_bytes=VMEM_LIMIT
        ),
        cost_estimate=pl.CostEstimate(flops=flops, bytes_accessed=2 ** 22, transcendentals=flops // 512),
    )(row_counts, queries, keys, values)


def solution(mesh):
    placed = (P(("blk", "uly"), None), P(("blk", "uly"), None), P(("blk", "uly"), None), P())
    return jax.shard_map(
        per_device,
        mesh=mesh,
        in_specs=placed,
        out_specs=(P(("blk", "uly"), None), P(("blk", "uly"), None)),
        check_vma=False,
    )
```

time: 362 us -> 70.3 us (0.19)
  waiting for transfers between devices: 170 us -> 0 us
  Pallas kernels: 0 us -> 65.9 us
  matrix products: 57.4 us -> 0 us
  blocking collectives: 44 us -> 0 us
  local copies, waits for them, and re-layouts: 32.9 us -> 2.35 us
  starting transfers between devices: 24.8 us -> 0 us
  between operations: 15.2 us -> 0.65 us
  other arithmetic: 14 us -> 0 us
    all_gather x4 -> x0, waiting for transfers between devices: 142 us -> none  [the longest x1 74.1 us: per_device(): lax.all_gather(head_v, 'blk', axis=0, tiled=True)]
    pallas_call x0 -> x1, Pallas kernels: none -> 65.9 us  [per_device(): pl.pallas_call(kernel, out_shape=(jax.ShapeDtypeStruct((TOK, NP * D), bf)...]
    dot_general x64 -> x0, matrix products: 57.4 us -> none  [the longest x32 29.7 us: online_update(): jnp.einsum('qhk,khd->qhd', expon.astype(jnp.bfloat16), value_block, prefe...]
    all_to_all x3 -> x0, blocking collectives: 44 us -> none  [the longest x1 18.6 us: per_device(): lax.all_to_all(main_k, 'uly', split_axis=1, concat_axis=0, tiled=True)]
    all_to_all x4 -> x0, waiting for transfers between devices: 28.1 us -> none  [the longest x1 14.7 us: per_device(): lax.all_to_all(rest_v, 'uly', split_axis=1, concat_axis=0, tiled=True)]
    dynamic_slice x33 -> x0, local copies, waits for them, and re-layouts: 25.3 us -> none  [the longest x32 25.1 us: fold_blocks(): state, unused = lax.scan(step_fn, state, (keys_split, values_split))]
    all_to_all x4 -> x0, starting transfers between devices: 24.7 us -> none  [the longest x1 13.7 us: per_device(): lax.all_to_all(main_q, 'uly', split_axis=1, concat_axis=0, tiled=True)]
    reduce_sum x33 -> x0, other arithmetic: 11.4 us -> none  [the longest x32 10.7 us: online_update(): totals = totals * factor + jnp.sum(expon, axis=2)]
  transfers between devices with their start and end apart: 8 -> 0, of which waited for: 6 -> 0; matrix products, arithmetic and copies ran while one was open for 28% -> 0% of each run, Pallas kernels for 0% -> 0%
where the time goes in v3:
time: 70.3 us; the launch traced here: 68.9 us
  Pallas kernels  65.9 us (94%)
  local copies, waits for them, and re-layouts  2.35 us (3%)
    pallas_call x1, Pallas kernels, per_device(): pl.pallas_call(kernel, out_shape=(jax.ShapeDtypeStruct((TOK, NP * D), bf)...  65.9 us
    unnamed x4, local copies, waits for them, and re-layouts  2.35 us

profile of v3, /device:TPU:1, one launch (start us, length us, event | category | flops | bytes accessed | tf_op | source)
XLA Modules:
  0.0 68.9 jit_solution(11589992543808603556)
XLA Ops:
  0.6 65.9 %shard_map.59 = (bf16[32,4096]{1,0:T(8,128)(2,1)}, bf16[448,128]{1,0:T(8,128)(2,1)}) custom-call(s32[16]{0:T(128)} %counts_ref.1, bf16[32,5120]{1,0:T(8,128)(2,1)} %q_ref.1, bf16[32,5120]{1,0:T(8,128)(2,1)} %k_ref.1, bf16[32,5120]{1,0:T(8,128)(2,1)} %v_ref.1), custom_call_target="tpu_custom_call" | custom-call | flops 5368709120 | bytes 4194304 | tf_op jit(solution)/shard_map/pallas_call | solution.py:452
  66.5 0.0 copy-start
  66.5 1.7 %copy.8 = bf16[32,4096]{1,0:T(8,128)(2,1)} copy(bf16[32,4096]{1,0:T(8,128)(2,1)} %get-tuple-element.4) | data formatting | bytes 524288
  68.3 0.0 copy-done
  68.3 0.6 copy.9
Async XLA Ops:
  66.5 1.7 %copy-start = (bf16[448,128]{1,0:T(8,128)(2,1)S(1)}, bf16[448,128]{1,0:T(8,128)(2,1)}, u32[]{:S(2)}) copy-start(bf16[448,128]{1,0:T(8,128)(2,1)} %get-tuple-element.5) | copy-start | bytes 344068

commit v4 on v3

--- a/solution.py
+++ b/solution.py
@@ -1,3 +1,5 @@
+import functools
+
 import jax
 import jax.numpy as jnp
 from jax import lax
@@ -11,7 +13,7 @@
 TOK = 32
 D = 128
 MOST = 448
-QB = 256
+QB = 128
 VMEM_LIMIT = 64 * 2 ** 20 - 2 ** 18
 EXP2_SCALE = D ** (-0.5) * 1.4426950408889634
 MESH = pl.DeviceIdType.MESH
@@ -285,67 +287,37 @@
     main_far(0)
     landed(qs.at[0], s1_recv.at[s_mq])
 
-    def ready_own(pair):
-        main_across(pair, 0)
-
-    def before_left():
-        main_far(1)
+    def queries_over_y():
         for i in range(1, NY):
             frm = lax.rem(y + i, NY)
             lq_copy(frm, frm).wait_recv()
 
-    def before_left_across():
-        lc_copy(1 - c).wait_recv()
-
     xs = (x, xl, xr, xf)
+    if pairs > 1:
+        early = [lambda: main_own(2)]
+        middle = [lambda: main_own(3), lambda: main_pass(2)]
+        late = [lambda: main_pass(3), lambda: main_far(2), lambda: main_across(1, 0)]
+    else:
+        early, middle, late = [], [], []
     plan = [
-        (0, x * pairs, lambda: main_across(0, 0)),
-        (1, left_slot + c, before_left),
-        (1, left_slot + 1 - c, before_left_across),
-    ]
-
-    def first_neighbour():
-        main_across(0, 1)
-        send_partial()
-
-    def second_neighbour():
-        main_across(0, 2)
-        if pairs > 1:
-            main_own(2)
-
-    def first_far():
-        main_across(0, 3)
-        if pairs > 1:
-            main_own(3)
-            main_pass(2)
-        else:
-            merge_left()
-
-    plan += [
-        (0, xl * pairs, first_neighbour),
-        (0, xr * pairs, second_neighbour),
-        (0, xf * pairs, first_far),
+        (0, x * pairs, [lambda: main_across(0, 0)]),
+        (1, left_slot + c, [lambda: main_far(1), queries_over_y]),
+        (1, left_slot + 1 - c, early + [lambda: lc_copy(1 - c).wait_recv()]),
+        (0, xl * pairs, [lambda: main_across(0, 1), send_partial]),
+        (0, xr * pairs, middle + [lambda: main_across(0, 2)]),
+        (0, xf * pairs, [lambda: main_across(0, 3)] + ([merge_left] if pairs == 1 else [])),
     ]
     if pairs > 1:
-        def second_own():
-            merge_left()
-            main_far(2)
-            main_across(1, 0)
-
-        def second_left():
-            main_pass(3)
-            main_across(1, 1)
-
-        def second_right():
-            main_far(3)
-            main_across(1, 2)
-
         plan += [
-            (0, x * pairs + 1, second_own),
-            (0, xl * pairs + 1, second_left),
-            (0, xr * pairs + 1, second_right),
-            (0, xf * pairs + 1, lambda: main_across(1, 3)),
+            (0, x * pairs + 1, late),
+            (0, xl * pairs + 1, [lambda: main_across(1, 1), merge_left]),
+            (0, xr * pairs + 1, [lambda: main_far(3), lambda: main_across(1, 2)]),
+            (0, xf * pairs + 1, [lambda: main_across(1, 3)]),
         ]
+
+    def run_all(events):
+        for event in events:
+            event()
 
     def chosen(t, values):
         out = values[0]
@@ -355,7 +327,7 @@
 
     def step(t, _):
         for i, (head, slot, first) in enumerate(plan[:-1]):
-            pl.when(t == i)(first)
+            pl.when(t == i)(functools.partial(run_all, first))
         attend(chosen(t, [p[0] for p in plan[:-1]]), chosen(t, [p[1] for p in plan[:-1]]))
         return 0
 
@@ -364,30 +336,29 @@
     def send_out(p):
         remote(out_main.at[p], columns(att_ref, me), om_send, om_recv, dev_p(p)).start()
 
-    plan[-1][2]()
-    parts = 2
+    run_all(plan[-1][2])
+    parts = min(4, NZ)
+    each = NZ // parts
+    turn = [d % NZ for d in ((4, 3, 5, 2, 6, 1, 7, 0) if NZ == 8 else (1, 0))]
 
     def last(j, _):
-        for i in range(rows // QB // parts):
-            blk = j * (rows // QB // parts) + i
-            at, now, total, weight = update(0, plan[-1][1], blk)
-            out_main[pl.ds(blk * (QB // TOK), QB // TOK)] = (
-                (total / weight).astype(jnp.bfloat16).reshape(QB // TOK, TOK, D))
-
-        def send(i, _):
-            p = j * (NP // parts) + i
-
-            @pl.when(p == me)
-            def _():
-                pltpu.make_async_copy(out_main.at[me], columns(att_ref, me), om_recv).start()
-
-            @pl.when(p != me)
-            def _():
-                send_out(p)
-
-            return 0
-
-        lax.fori_loop(0, NP // parts, send, 0)
+        planes = [lax.rem(z + chosen(j, turn[i::each]), NZ) for i in range(each)]
+        for plane in planes:
+            at, now, total, weight = update(0, plan[-1][1], plane)
+            out_main[pl.ds(plane * NY, NY)] = (total / weight).astype(jnp.bfloat16).reshape(NY, TOK, D)
+        for plane in planes:
+            for i in range(NY):
+                p = plane * NY + lax.rem(y + i, NY)
+                if i > 0:
+                    send_out(p)
+                else:
+                    @pl.when(p == me)
+                    def _():
+                        pltpu.make_async_copy(out_main.at[me], columns(att_ref, me), om_recv).start()
+
+                    @pl.when(p != me)
+                    def _():
+                        send_out(p)
         return 0
 
     lax.fori_loop(0, parts, last, 0)

time: 70.3 us -> 66.5 us (0.946); the launches traced: 68.9 us -> 66.4 us
  Pallas kernels: 65.9 us -> 63.4 us
    pallas_call x1, Pallas kernels: 65.9 us -> 63.4 us  [per_device(): pl.pallas_call(kernel, out_shape=(jax.ShapeDtypeStruct((TOK, NP * D), bf)...]
where the time goes in v4:
time: 66.5 us; the launch traced here: 66.4 us
  Pallas kernels  63.4 us (95%)
  local copies, waits for them, and re-layouts  2.35 us (4%)
    pallas_call x1, Pallas kernels, per_device(): pl.pallas_call(kernel, out_shape=(jax.ShapeDtypeStruct((TOK, NP * D), bf)...  63.4 us
    unnamed x4, local copies, waits for them, and re-layouts  2.35 us

profile of v4, /device:TPU:1, one launch (start us, length us, event | category | flops | bytes accessed | tf_op | source)
XLA Modules:
  0.0 66.4 jit_solution(8264752522569097327)
XLA Ops:
  0.6 63.4 %shard_map.59 = (bf16[32,4096]{1,0:T(8,128)(2,1)}, bf16[448,128]{1,0:T(8,128)(2,1)}) custom-call(s32[16]{0:T(128)} %counts_ref.1, bf16[32,5120]{1,0:T(8,128)(2,1)} %q_ref.1, bf16[32,5120]{1,0:T(8,128)(2,1)} %k_ref.1, bf16[32,5120]{1,0:T(8,128)(2,1)} %v_ref.1), custom_call_target="tpu_custom_call" | custom-call | flops 5368709120 | bytes 4194304 | tf_op jit(solution)/shard_map/pallas_call | solution.py:423
  64.0 0.0 copy-start
  64.0 1.7 %copy.8 = bf16[32,4096]{1,0:T(8,128)(2,1)} copy(bf16[32,4096]{1,0:T(8,128)(2,1)} %get-tuple-element.4) | data formatting | bytes 524288
  65.7 0.0 copy-done
  65.7 0.6 copy.9
Async XLA Ops:
  64.0 1.7 %copy-start = (bf16[448,128]{1,0:T(8,128)(2,1)S(1)}, bf16[448,128]{1,0:T(8,128)(2,1)}, u32[]{:S(2)}) copy-start(bf16[448,128]{1,0:T(8,128)(2,1)} %get-tuple-element.5) | copy-start | bytes 344068

commit v5 on v4

--- a/solution.py
+++ b/solution.py
@@ -19,11 +19,29 @@
 MESH = pl.DeviceIdType.MESH
 
 
+DIRECT = (2, 3, 4)
+
+
+def layout():
+    if NZ == 8:
+        order = (0, 1, -1, 2, 3, -2, 4, -3)
+        sizes = ((2, 2), (2, 1, 1))
+    else:
+        order, sizes = (0, 1), ((1, 1),)
+    chunks = []
+    for slot, each in enumerate(sizes):
+        first = 0
+        for n in each:
+            chunks.append((slot, first, n * NY))
+            first += 2 * n * NY
+    return order, chunks, len(sizes)
+
+
 def kernel(
     counts_ref, q_ref, k_ref, v_ref, att_ref, left_ref,
     kv, qs, acc, top, out_main, part_o, part_s, got_o, got_s, out_left, got_left,
     s1_send, s1_recv, m_send, m_recv, mc_send, mc_recv, lx_send, lx_recv, lc_send, lc_recv,
-    lq_send, lq_recv, lp_send, lp_recv, lo_send, lo_recv, om_send, om_recv,
+    lq_send, lq_recv, lp_send, lp_recv, lo_send, lo_recv, om_send, om_recv, ready,
 ):
     u = lax.axis_index("uly")
     b = lax.axis_index("blk")
@@ -34,13 +52,13 @@
     zh = b // (2 * NX)
     z = zh * ZL + zl
     me = z * NY + y
-    chunks = 4 if NZ == 8 else 2
-    order = (0, 1, -1, 2, 3, -2, 4, -3) if NZ == 8 else (0, 1)
-    per = NP // chunks
-    pairs = chunks // 2
+    order, parts_of, pairs = layout()
+    chunks = len(parts_of)
+    direct = DIRECT
     rows = NP * TOK
     group = NZ * TOK
     left_slot = NX * pairs
+    keys = kv.shape[1] * TOK
 
     def dev(x_, c_, z_, y_):
         return {"uly": lax.rem(z_, ZL) * NY + y_, "blk": ((z_ // ZL) * NX + x_) * 2 + c_}
@@ -59,11 +77,13 @@
     barrier = pltpu.get_barrier_semaphore()
 
     def greet(i, _):
-        pl.semaphore_signal(barrier, inc=1, device_id=dev_p(lax.rem(me + i, NP)), device_id_type=MESH)
-        return 0
-
-    lax.fori_loop(1, NP, greet, 0)
-    for to in (dev(xr, c, z, y), dev(xl, c, z, y), dev(x, 1 - c, z, y)):
+        pl.semaphore_signal(barrier, inc=1, device_id=dev(x, c, lax.rem(z + i, NZ), y), device_id_type=MESH)
+        return 0
+
+    lax.fori_loop(1, NZ, greet, 0)
+    row = [dev(x, c, z, lax.rem(y + i, NY)) for i in range(1, NY)]
+    near = [dev(xr, c, z, y), dev(xl, c, z, y), dev(xf, c, z, y), dev(x, 1 - c, z, y)]
+    for to in row + near:
         pl.semaphore_signal(barrier, inc=1, device_id=to, device_id_type=MESH)
 
     def columns(ref, head):
@@ -72,16 +92,18 @@
     def left_head(zz):
         return NP + lax.rem(zz, ZL) * (NY // 2) + zz // ZL
 
-    s_left, s_mq, s_lq = 4, 5, 6
+    s_left, s_mq, s_lq = chunks, chunks + 1, chunks + 2
 
     def main_rows(xx, k, cc, lo, n):
-        return kv.at[xx * pairs + k // 2, pl.ds((k % 2) * 2 * per + cc * per + lo, n)]
+        slot, first, size = parts_of[k]
+        return kv.at[xx * pairs + slot, pl.ds(first + cc * size + lo, n)]
 
     def left_rows(cc, xx, lo, n):
         return kv.at[left_slot + cc, pl.ds(xx * NZ + lo, n)]
 
     def place_main(k, src, n):
-        return kv.at[x * pairs + k // 2, (k % 2) * 2 * per + c * per + src, pl.ds(n * TOK, TOK)]
+        slot, first, size = parts_of[k]
+        return kv.at[x * pairs + slot, first + c * size + src, pl.ds(n * TOK, TOK)]
 
     def place_left(n):
         return kv.at[left_slot + c, x * NZ + z, pl.ds(n * TOK, TOK)]
@@ -98,7 +120,9 @@
         copy.start()
     acc[...] = jnp.zeros_like(acc)
     top[...] = jnp.full_like(top, -1e30)
-    pl.semaphore_wait(barrier, NP - 1 + 3)
+    pl.semaphore_wait(barrier, NZ - 1 + len(row) + len(near))
+    for to in row:
+        pl.semaphore_signal(ready, inc=1, device_id=to, device_id_type=MESH)
 
     def send_lkv(i, _):
         to = lax.rem(z + i, NZ)
@@ -114,9 +138,10 @@
         return 0
 
     def send_mkv(k):
-        for rel in range(k * per // NY, (k + 1) * per // NY):
+        before = sum(part[2] for part in parts_of[:k]) // NY
+        for rel in range(before, before + parts_of[k][2] // NY):
             to_z = lax.rem(z - order[rel] + NZ, NZ)
-            slot = (rel % (per // NY)) * NY + y
+            slot = (rel - before) * NY + y
 
             def send(i, _):
                 to_y = lax.rem(y + i, NY)
@@ -133,28 +158,29 @@
         return 0
 
     lax.fori_loop(1, NZ, send_lkv, 0)
-    for k in range(chunks // 2):
+    pl.semaphore_wait(ready, len(row))
+    for k in range(2):
         send_mkv(k)
     lax.fori_loop(1, NZ, send_lq, 0)
     lax.fori_loop(1, NP, send_mq, 0)
-    for k in range(chunks // 2, chunks):
+    for k in range(2, chunks):
         send_mkv(k)
 
     def landed(ref, sem):
         pltpu.make_async_copy(ref, ref, sem).wait()
 
     def m_copy(k, kind, xx, to):
-        lo, n = ((0, per), (0, per), (0, per // 2), (per // 2, per // 2))[kind]
+        size = parts_of[k][2]
+        lo, n = ((0, size), (0, size), (0, size // 2), (size // 2, size // 2), (0, size))[kind]
         part = main_rows(xx, k, c, lo, n)
         return remote(part, part, m_send.at[k, kind], m_recv.at[k, kind], dev(to, c, z, y))
 
     def mc_copy(k, i, cc, xx):
-        part = main_rows(xx, k, cc, 0, per)
+        part = main_rows(xx, k, cc, 0, parts_of[k][2])
         return remote(part, part, mc_send.at[k, i], mc_recv.at[k, i], dev(x, 1 - c, z, y))
 
     def lx_copy(kind, xx, to):
-        lo, n = ((0, NZ), (0, NZ), (0, NZ // 2), (NZ // 2, NZ // 2))[kind]
-        part = left_rows(c, xx, lo, n)
+        part = left_rows(c, xx, 0, NZ)
         return remote(part, part, lx_send.at[kind], lx_recv.at[kind], dev(to, c, z, y))
 
     def lc_copy(cc):
@@ -173,27 +199,35 @@
         ]
 
     def main_own(k):
-        landed(main_rows(x, k, c, 0, per), s1_recv.at[k])
+        landed(main_rows(x, k, c, 0, parts_of[k][2]), s1_recv.at[k])
         m_copy(k, 0, x, xr).start()
         m_copy(k, 1, x, xl).start()
+        if k in direct:
+            m_copy(k, 4, x, xf).start()
         mc_copy(k, 0, c, x).start()
 
     def main_pass(k):
         m_copy(k, 0, xl, xr).wait_recv()
-        m_copy(k, 2, xl, xr).start()
+        if k not in direct:
+            m_copy(k, 2, xl, xr).start()
         mc_copy(k, 1, c, xl).start()
         m_copy(k, 1, xr, xl).wait_recv()
-        m_copy(k, 3, xr, xl).start()
+        if k not in direct:
+            m_copy(k, 3, xr, xl).start()
         mc_copy(k, 2, c, xr).start()
 
     def main_far(k):
-        m_copy(k, 2, xf, xr).wait_recv()
-        m_copy(k, 3, xf, xl).wait_recv()
+        if k in direct:
+            m_copy(k, 4, xf, xf).wait_recv()
+        else:
+            m_copy(k, 2, xf, xr).wait_recv()
+            m_copy(k, 3, xf, xl).wait_recv()
         mc_copy(k, 3, c, xf).start()
 
     def main_across(pair, i):
-        for k in (2 * pair, 2 * pair + 1):
-            mc_copy(k, i, 1 - c, (x, xl, xr, xf)[i]).wait_recv()
+        for k, part in enumerate(parts_of):
+            if part[0] == pair:
+                mc_copy(k, i, 1 - c, (x, xl, xr, xf)[i]).wait_recv()
 
     def update(head, slot, i):
         at = pl.multiple_of(i * QB, QB)
@@ -201,8 +235,8 @@
             at = pl.multiple_of(head * rows + at, QB)
         n = QB // TOK
         qq = qs[head, pl.ds(i * n, n)].reshape(QB, D)
-        kk = kv[slot, :, 0:TOK, :].reshape(4 * per * TOK, D)
-        vv = kv[slot, :, TOK:2 * TOK, :].reshape(4 * per * TOK, D)
+        kk = kv[slot, :, 0:TOK, :].reshape(keys, D)
+        vv = kv[slot, :, TOK:2 * TOK, :].reshape(keys, D)
         s = lax.dot_general(qq, kk, (((1,), (1,)), ((), ())), preferred_element_type=jnp.float32)
         before = top[pl.ds(at, QB), :]
         now = jnp.maximum(before, jnp.max(s, axis=1, keepdims=True))
@@ -269,19 +303,17 @@
     landed(left_rows(c, x, 0, NZ), s1_recv.at[s_left])
     lx_copy(0, x, xr).start()
     lx_copy(1, x, xl).start()
+    lx_copy(2, x, xf).start()
     main_own(0)
-    lx_copy(0, xl, xr).wait_recv()
-    lx_copy(2, xl, xr).start()
-    lx_copy(1, xr, xl).wait_recv()
-    lx_copy(3, xr, xl).start()
     main_own(1)
     landed(qs.at[1, pl.ds(y * NZ, NZ)], s1_recv.at[s_lq])
     for i in range(1, NY):
         to = lax.rem(y + i, NY)
         lq_copy(y, to).start()
     main_pass(0)
-    lx_copy(2, xf, xr).wait_recv()
-    lx_copy(3, xf, xl).wait_recv()
+    lx_copy(0, xl, xr).wait_recv()
+    lx_copy(1, xr, xl).wait_recv()
+    lx_copy(2, xf, xf).wait_recv()
     lc_copy(c).start()
     main_pass(1)
     main_far(0)
@@ -294,24 +326,24 @@
 
     xs = (x, xl, xr, xf)
     if pairs > 1:
-        early = [lambda: main_own(2)]
-        middle = [lambda: main_own(3), lambda: main_pass(2)]
-        late = [lambda: main_pass(3), lambda: main_far(2), lambda: main_across(1, 0)]
+        soon, early = [lambda: main_own(2)], [lambda: main_own(3)]
+        middle = [lambda: main_own(4)]
+        late = [lambda: main_pass(2), lambda: main_far(2), lambda: main_pass(3), lambda: main_across(1, 0)]
     else:
-        early, middle, late = [], [], []
+        soon, early, middle, late = [], [], [], []
     plan = [
         (0, x * pairs, [lambda: main_across(0, 0)]),
-        (1, left_slot + c, [lambda: main_far(1), queries_over_y]),
-        (1, left_slot + 1 - c, early + [lambda: lc_copy(1 - c).wait_recv()]),
-        (0, xl * pairs, [lambda: main_across(0, 1), send_partial]),
+        (1, left_slot + c, [lambda: main_far(1), queries_over_y] + soon),
+        (1, left_slot + 1 - c, [lambda: lc_copy(1 - c).wait_recv()]),
+        (0, xl * pairs, [lambda: main_across(0, 1), send_partial] + early),
         (0, xr * pairs, middle + [lambda: main_across(0, 2)]),
         (0, xf * pairs, [lambda: main_across(0, 3)] + ([merge_left] if pairs == 1 else [])),
     ]
     if pairs > 1:
         plan += [
             (0, x * pairs + 1, late),
-            (0, xl * pairs + 1, [lambda: main_across(1, 1), merge_left]),
-            (0, xr * pairs + 1, [lambda: main_far(3), lambda: main_across(1, 2)]),
+            (0, xl * pairs + 1, [lambda: main_pass(4), merge_left, lambda: main_across(1, 1)]),
+            (0, xr * pairs + 1, [lambda: main_far(3), lambda: main_far(4), lambda: main_across(1, 2)]),
             (0, xf * pairs + 1, [lambda: main_across(1, 3)]),
         ]
 
@@ -388,14 +420,16 @@
     for k in range(chunks):
         m_copy(k, 0, x, xr).wait_send()
         m_copy(k, 1, x, xl).wait_send()
-        m_copy(k, 2, xl, xr).wait_send()
-        m_copy(k, 3, xr, xl).wait_send()
+        if k in direct:
+            m_copy(k, 4, x, xf).wait_send()
+        else:
+            m_copy(k, 2, xl, xr).wait_send()
+            m_copy(k, 3, xr, xl).wait_send()
         for i in range(4):
             mc_copy(k, i, c, xs[i]).wait_send()
     lx_copy(0, x, xr).wait_send()
     lx_copy(1, x, xl).wait_send()
-    lx_copy(2, xl, xr).wait_send()
-    lx_copy(3, xr, xl).wait_send()
+    lx_copy(2, x, xf).wait_send()
     lc_copy(c).wait_send()
     for i in range(1, NY):
         to = lax.rem(y + i, NY)
@@ -414,12 +448,14 @@
 def per_device(queries, keys, values, row_counts):
     vmem = pl.BlockSpec(memory_space=pltpu.VMEM)
     hbm = pl.BlockSpec(memory_space=pltpu.HBM)
-    chunks = 4 if NZ == 8 else 2
+    order, parts_of, pairs = layout()
+    chunks = len(parts_of)
+    slots = NX * pairs + 2
     rows = NP * TOK
     group = NZ * TOK
     dma = pltpu.SemaphoreType.DMA
     bf, f32 = jnp.bfloat16, jnp.float32
-    flops = 4 * rows * (NX * chunks // 2 + 2) * rows * D
+    flops = 4 * rows * slots * rows * D
     return pl.pallas_call(
         kernel,
         out_shape=(
@@ -429,7 +465,7 @@
         in_specs=[pl.BlockSpec(memory_space=pltpu.SMEM), hbm, hbm, hbm],
         out_specs=(hbm, vmem),
         scratch_shapes=[
-            pltpu.VMEM((NX * chunks // 2 + 2, 4 * NP // chunks, 2 * TOK, D), bf),
+            pltpu.VMEM((slots, NX * NZ, 2 * TOK, D), bf),
             pltpu.VMEM((2, NP, TOK, D), bf),
             pltpu.VMEM((2 * rows, 2 * D), f32),
             pltpu.VMEM((2 * rows, D), f32),
@@ -440,9 +476,9 @@
             pltpu.VMEM((NY, group, D), f32),
             pltpu.VMEM((NZ, TOK, D), bf),
             pltpu.VMEM((NY, ZL, TOK, D), bf),
-            dma((5,)), dma((7,)), dma((4, 4)), dma((4, 4)), dma((4, 4)), dma((4, 4)),
-            dma((4,)), dma((4,)), dma, dma,
-            dma((NY,)), dma((NY,)), dma((2, NY)), dma((2, NY)), dma((2 * ZH,)), dma((NY,)), dma, dma,
+            dma((5,)), dma((chunks + 3,)), dma((chunks, 5)), dma((chunks, 5)), dma((chunks, 4)), dma((chunks, 4)),
+            dma((3,)), dma((3,)), dma, dma,
+            dma((NY,)), dma((NY,)), dma((2, NY)), dma((2, NY)), dma((2 * ZH,)), dma((NY,)), dma, dma, pltpu.SemaphoreType.REGULAR,
         ],
         compiler_params=pltpu.CompilerParams(
             collective_id=0, has_side_effects=True, vmem_limit_bytes=VMEM_LIMIT

time: 66.5 us -> 67.2 us (1.011)
  Pallas kernels: 63.4 us -> 64.1 us
    pallas_call x1, Pallas kernels: 63.4 us -> 64.1 us  [per_device(): pl.pallas_call(kernel, out_shape=(jax.ShapeDtypeStruct((TOK, NP * D), bf)...]
where the time goes in v5:
time: 67.2 us; the launch traced here: 67.1 us
  Pallas kernels  64.1 us (95%)
  local copies, waits for them, and re-layouts  2.35 us (3%)
    pallas_call x1, Pallas kernels, per_device(): pl.pallas_call(kernel, out_shape=(jax.ShapeDtypeStruct((TOK, NP * D), bf)...  64.1 us
    unnamed x4, local copies, waits for them, and re-layouts  2.35 us

profile of v5, /device:TPU:1, one launch (start us, length us, event | category | flops | bytes accessed | tf_op | source)
XLA Modules:
  0.0 67.1 jit_solution(9393315333317910286)
XLA Ops:
  0.6 64.1 %shard_map.59 = (bf16[32,4096]{1,0:T(8,128)(2,1)}, bf16[448,128]{1,0:T(8,128)(2,1)}) custom-call(s32[16]{0:T(128)} %counts_ref.1, bf16[32,5120]{1,0:T(8,128)(2,1)} %q_ref.1, bf16[32,5120]{1,0:T(8,128)(2,1)} %k_ref.1, bf16[32,5120]{1,0:T(8,128)(2,1)} %v_ref.1), custom_call_target="tpu_custom_call" | custom-call | flops 5368709120 | bytes 4194304 | tf_op jit(solution)/shard_map/pallas_call | solution.py:459
  64.8 0.0 copy-start
  64.8 1.7 %copy.8 = bf16[32,4096]{1,0:T(8,128)(2,1)} copy(bf16[32,4096]{1,0:T(8,128)(2,1)} %get-tuple-element.4) | data formatting | bytes 524288
  66.5 0.0 copy-done
  66.5 0.6 copy.9
Async XLA Ops:
  64.8 1.7 %copy-start = (bf16[448,128]{1,0:T(8,128)(2,1)S(1)}, bf16[448,128]{1,0:T(8,128)(2,1)}, u32[]{:S(2)}) copy-start(bf16[448,128]{1,0:T(8,128)(2,1)} %get-tuple-element.5) | copy-start | bytes 344068

commit v6 on v5

--- a/solution.py
+++ b/solution.py
@@ -19,7 +19,7 @@
 MESH = pl.DeviceIdType.MESH
 
 
-DIRECT = (2, 3, 4)
+DIRECT = ()
 
 
 def layout():
@@ -162,8 +162,10 @@
     for k in range(2):
         send_mkv(k)
     lax.fori_loop(1, NZ, send_lq, 0)
+    for k in range(2, min(3, chunks)):
+        send_mkv(k)
     lax.fori_loop(1, NP, send_mq, 0)
-    for k in range(2, chunks):
+    for k in range(3, chunks):
         send_mkv(k)
 
     def landed(ref, sem):
@@ -317,7 +319,6 @@
     lc_copy(c).start()
     main_pass(1)
     main_far(0)
-    landed(qs.at[0], s1_recv.at[s_mq])
 
     def queries_over_y():
         for i in range(1, NY):
@@ -325,25 +326,24 @@
             lq_copy(frm, frm).wait_recv()
 
     xs = (x, xl, xr, xf)
-    if pairs > 1:
-        soon, early = [lambda: main_own(2)], [lambda: main_own(3)]
-        middle = [lambda: main_own(4)]
-        late = [lambda: main_pass(2), lambda: main_far(2), lambda: main_pass(3), lambda: main_across(1, 0)]
-    else:
-        soon, early, middle, late = [], [], [], []
+    def main_queries():
+        landed(qs.at[0], s1_recv.at[s_mq])
+
+    several = pairs > 1
     plan = [
-        (0, x * pairs, [lambda: main_across(0, 0)]),
-        (1, left_slot + c, [lambda: main_far(1), queries_over_y] + soon),
-        (1, left_slot + 1 - c, [lambda: lc_copy(1 - c).wait_recv()]),
-        (0, xl * pairs, [lambda: main_across(0, 1), send_partial] + early),
-        (0, xr * pairs, middle + [lambda: main_across(0, 2)]),
-        (0, xf * pairs, [lambda: main_across(0, 3)] + ([merge_left] if pairs == 1 else [])),
+        (1, left_slot + c, [queries_over_y]),
+        (1, left_slot + 1 - c, [lambda: main_own(2)] * several + [lambda: lc_copy(1 - c).wait_recv()]),
+        (0, x * pairs, [lambda: main_far(1), send_partial, main_queries, lambda: main_across(0, 0)]),
+        (0, xl * pairs, [lambda: main_own(3), lambda: main_pass(2)] * several + [lambda: main_across(0, 1)]),
+        (0, xr * pairs, [lambda: main_own(4), lambda: main_far(2)] * several + [lambda: main_across(0, 2)]),
+        (0, xf * pairs, [lambda: main_pass(3)] * several + [merge_left] * (not several)
+         + [lambda: main_across(0, 3)]),
     ]
-    if pairs > 1:
+    if several:
         plan += [
-            (0, x * pairs + 1, late),
-            (0, xl * pairs + 1, [lambda: main_pass(4), merge_left, lambda: main_across(1, 1)]),
-            (0, xr * pairs + 1, [lambda: main_far(3), lambda: main_far(4), lambda: main_across(1, 2)]),
+            (0, x * pairs + 1, [lambda: main_pass(4), lambda: main_far(3), lambda: main_across(1, 0)]),
+            (0, xl * pairs + 1, [lambda: main_far(4), merge_left, lambda: main_across(1, 1)]),
+            (0, xr * pairs + 1, [lambda: main_across(1, 2)]),
             (0, xf * pairs + 1, [lambda: main_across(1, 3)]),
         ]
 

time: 67.2 us -> 66.9 us (level)
  the two profiles are of different devices: /device:TPU:1 before, /device:TPU:32 now
where the time goes in v6:
time: 66.9 us; the launch traced here: 66.8 us
  Pallas kernels  63.8 us (95%)
  local copies, waits for them, and re-layouts  2.35 us (4%)
    pallas_call x1, Pallas kernels, per_device(): pl.pallas_call(kernel, out_shape=(jax.ShapeDtypeStruct((TOK, NP * D), bf)...  63.8 us
    unnamed x4, local copies, waits for them, and re-layouts  2.35 us

profile of v6, /device:TPU:32, one launch (start us, length us, event | category | flops | bytes accessed | tf_op | source)
XLA Modules:
  0.0 66.8 jit_solution(16958331676751582112)
XLA Ops:
  0.6 63.8 %shard_map.59 = (bf16[32,4096]{1,0:T(8,128)(2,1)}, bf16[448,128]{1,0:T(8,128)(2,1)}) custom-call(s32[16]{0:T(128)} %counts_ref.1, bf16[32,5120]{1,0:T(8,128)(2,1)} %q_ref.1, bf16[32,5120]{1,0:T(8,128)(2,1)} %k_ref.1, bf16[32,5120]{1,0:T(8,128)(2,1)} %v_ref.1), custom_call_target="tpu_custom_call" | custom-call | flops 5368709120 | bytes 4194304 | tf_op jit(solution)/shard_map/pallas_call | solution.py:459
  64.5 0.0 copy-start
  64.5 1.7 %copy.8 = bf16[32,4096]{1,0:T(8,128)(2,1)} copy(bf16[32,4096]{1,0:T(8,128)(2,1)} %get-tuple-element.4) | data formatting | bytes 524288
  66.2 0.0 copy-done
  66.2 0.6 copy.9
Async XLA Ops:
  64.5 1.7 %copy-start = (bf16[448,128]{1,0:T(8,128)(2,1)S(1)}, bf16[448,128]{1,0:T(8,128)(2,1)}, u32[]{:S(2)}) copy-start(bf16[448,128]{1,0:T(8,128)(2,1)} %get-tuple-element.5) | copy-start | bytes 344068

commit v7 on v6

--- a/solution.py
+++ b/solution.py
@@ -25,7 +25,7 @@
 def layout():
     if NZ == 8:
         order = (0, 1, -1, 2, 3, -2, 4, -3)
-        sizes = ((2, 2), (2, 1, 1))
+        sizes = ((2, 2), (2, 2))
     else:
         order, sizes = (0, 1), ((1, 1),)
     chunks = []
@@ -152,19 +152,27 @@
 
             lax.fori_loop(1 if rel == 0 else 0, NY, send, 0)
 
-    def send_mq(i, _):
-        to = lax.rem(me + i, NP)
-        remote(columns(q_ref, to), qs.at[0, me], s1_send.at[4], s1_recv.at[s_mq], dev_p(to)).start()
-        return 0
-
-    lax.fori_loop(1, NZ, send_lkv, 0)
+    turns = (1, 7, 2, 6, 3, 5, 4) if NZ == 8 else (1,)
+
+    def send_mq(plane):
+        def send(i, _):
+            to = lax.rem(z + plane, NZ) * NY + lax.rem(y + i, NY)
+            remote(columns(q_ref, to), qs.at[0, me], s1_send.at[4], s1_recv.at[s_mq], dev_p(to)).start()
+            return 0
+
+        lax.fori_loop(1 if plane == 0 else 0, NY, send, 0)
+
+    for plane in turns:
+        send_lkv(plane, 0)
     pl.semaphore_wait(ready, len(row))
     for k in range(2):
         send_mkv(k)
-    lax.fori_loop(1, NZ, send_lq, 0)
+    for plane in turns:
+        send_lq(plane, 0)
     for k in range(2, min(3, chunks)):
         send_mkv(k)
-    lax.fori_loop(1, NP, send_mq, 0)
+    for plane in turns[::-1] + (0,):
+        send_mq(plane)
     for k in range(3, chunks):
         send_mkv(k)
 
@@ -335,14 +343,14 @@
         (1, left_slot + 1 - c, [lambda: main_own(2)] * several + [lambda: lc_copy(1 - c).wait_recv()]),
         (0, x * pairs, [lambda: main_far(1), send_partial, main_queries, lambda: main_across(0, 0)]),
         (0, xl * pairs, [lambda: main_own(3), lambda: main_pass(2)] * several + [lambda: main_across(0, 1)]),
-        (0, xr * pairs, [lambda: main_own(4), lambda: main_far(2)] * several + [lambda: main_across(0, 2)]),
+        (0, xr * pairs, [lambda: main_far(2)] * several + [lambda: main_across(0, 2)]),
         (0, xf * pairs, [lambda: main_pass(3)] * several + [merge_left] * (not several)
          + [lambda: main_across(0, 3)]),
     ]
     if several:
         plan += [
-            (0, x * pairs + 1, [lambda: main_pass(4), lambda: main_far(3), lambda: main_across(1, 0)]),
-            (0, xl * pairs + 1, [lambda: main_far(4), merge_left, lambda: main_across(1, 1)]),
+            (0, x * pairs + 1, [lambda: main_across(1, 0)]),
+            (0, xl * pairs + 1, [lambda: main_far(3), merge_left, lambda: main_across(1, 1)]),
             (0, xr * pairs + 1, [lambda: main_across(1, 2)]),
             (0, xf * pairs + 1, [lambda: main_across(1, 3)]),
         ]

time: 66.9 us -> 65.7 us (0.982)
  Pallas kernels: 63.8 us -> 62.6 us
    pallas_call x1, Pallas kernels: 63.8 us -> 62.6 us  [per_device(): pl.pallas_call(kernel, out_shape=(jax.ShapeDtypeStruct((TOK, NP * D), bf)...]
where the time goes in v7:
time: 65.7 us; the launch traced here: 65.6 us
  Pallas kernels  62.6 us (95%)
  local copies, waits for them, and re-layouts  2.35 us (4%)
    pallas_call x1, Pallas kernels, per_device(): pl.pallas_call(kernel, out_shape=(jax.ShapeDtypeStruct((TOK, NP * D), bf)...  62.6 us
    unnamed x4, local copies, waits for them, and re-layouts  2.35 us

profile of v7, /device:TPU:32, one launch (start us, length us, event | category | flops | bytes accessed | tf_op | source)
XLA Modules:
  0.0 65.6 jit_solution(1584783233544413460)
XLA Ops:
  0.6 62.6 %shard_map.59 = (bf16[32,4096]{1,0:T(8,128)(2,1)}, bf16[448,128]{1,0:T(8,128)(2,1)}) custom-call(s32[16]{0:T(128)} %counts_ref.1, bf16[32,5120]{1,0:T(8,128)(2,1)} %q_ref.1, bf16[32,5120]{1,0:T(8,128)(2,1)} %k_ref.1, bf16[32,5120]{1,0:T(8,128)(2,1)} %v_ref.1), custom_call_target="tpu_custom_call" | custom-call | flops 5368709120 | bytes 4194304 | tf_op jit(solution)/shard_map/pallas_call | solution.py:467
  63.2 0.0 copy-start
  63.3 1.7 %copy.8 = bf16[32,4096]{1,0:T(8,128)(2,1)} copy(bf16[32,4096]{1,0:T(8,128)(2,1)} %get-tuple-element.4) | data formatting | bytes 524288
  65.0 0.0 copy-done
  65.0 0.6 copy.9
Async XLA Ops:
  63.2 1.7 %copy-start = (bf16[448,128]{1,0:T(8,128)(2,1)S(1)}, bf16[448,128]{1,0:T(8,128)(2,1)}, u32[]{:S(2)}) copy-start(bf16[448,128]{1,0:T(8,128)(2,1)} %get-tuple-element.5) | copy-start | bytes 344068

commit v8 on v7

--- a/solution.py
+++ b/solution.py
@@ -24,8 +24,8 @@
 
 def layout():
     if NZ == 8:
-        order = (0, 1, -1, 2, 3, -2, 4, -3)
-        sizes = ((2, 2), (2, 2))
+        order = (0, 1, -1, 2, 3, -2, -3, 4)
+        sizes = ((2, 2), (3, 1))
     else:
         order, sizes = (0, 1), ((1, 1),)
     chunks = []

time: 65.7 us -> 66.8 us (1.017)
  Pallas kernels: 62.6 us -> 63.7 us
    pallas_call x1, Pallas kernels: 62.6 us -> 63.7 us  [per_device(): pl.pallas_call(kernel, out_shape=(jax.ShapeDtypeStruct((TOK, NP * D), bf)...]
where the time goes in v8:
time: 66.8 us; the launch traced here: 66.7 us
  Pallas kernels  63.7 us (95%)
  local copies, waits for them, and re-layouts  2.35 us (4%)
    pallas_call x1, Pallas kernels, per_device(): pl.pallas_call(kernel, out_shape=(jax.ShapeDtypeStruct((TOK, NP * D), bf)...  63.7 us
    unnamed x4, local copies, waits for them, and re-layouts  2.35 us

profile of v8, /device:TPU:32, one launch (start us, length us, event | category | flops | bytes accessed | tf_op | source)
XLA Modules:
  0.0 66.7 jit_solution(2600444646118398353)
XLA Ops:
  0.6 63.7 %shard_map.59 = (bf16[32,4096]{1,0:T(8,128)(2,1)}, bf16[448,128]{1,0:T(8,128)(2,1)}) custom-call(s32[16]{0:T(128)} %counts_ref.1, bf16[32,5120]{1,0:T(8,128)(2,1)} %q_ref.1, bf16[32,5120]{1,0:T(8,128)(2,1)} %k_ref.1, bf16[32,5120]{1,0:T(8,128)(2,1)} %v_ref.1), custom_call_target="tpu_custom_call" | custom-call | flops 5368709120 | bytes 4194304 | tf_op jit(solution)/shard_map/pallas_call | solution.py:467
  64.4 0.0 copy-start
  64.4 1.7 %copy.8 = bf16[32,4096]{1,0:T(8,128)(2,1)} copy(bf16[32,4096]{1,0:T(8,128)(2,1)} %get-tuple-element.4) | data formatting | bytes 524288
  66.1 0.0 copy-done
  66.1 0.6 copy.9
Async XLA Ops:
  64.4 1.7 %copy-start = (bf16[448,128]{1,0:T(8,128)(2,1)S(1)}, bf16[448,128]{1,0:T(8,128)(2,1)}, u32[]{:S(2)}) copy-start(bf16[448,128]{1,0:T(8,128)(2,1)} %get-tuple-element.5) | copy-start | bytes 344068
